TPU v7x, 32 devices: a whole 2x2x4 slice. The times are simulated.
32 devices in a mesh: rows: 8 (over z, y), feat: 4 (over x, core).
Axes of the slice: x: 2, y: 2, z: 4, core: 2. Of those that a mesh axis runs over, the one named last changes fastest.
Arguments:
- targets: bfloat16 [32768, 1024], P('rows', 'feat'), may hold values from -6 to 6
- omega: bfloat16 [1024, 256], P('feat'), may hold values from -0.1875 to 0.1875
- phase: float32 [256], replicated, may hold values from -3.140625 to 3.140625
- codes: int32 [32768, 128], P('rows', 'feat'), may hold values from 0 to 31, as said below
- node: int32 [32768], P('rows'), may hold values from 0 to 7, as said below
- boot_counts: int32 [32768], P('rows'), may hold values from 0 to 3
Outputs:
- gains: float32 [1024, 31], P(('feat', 'rows'))
- best: float32 [8], replicated
Inputs may be any that keep to these rules, and one draw needn't show every extreme that they name: `codes`: each feature has a lowest and a highest used bin; some features use bin 0 and some bin 32 - 1. Among the rows of each device every node holds a row with a nonzero bootstrap count.
All inputs are finite; a program needn't handle non-finite values.
Results may differ from a plain program's by a relative error of at most 0.00051.
Values may be sent and summed in bfloat16 or wider, within the bound.
No kernel may reach another device: no remote copies, remote signals or barrier semaphores. Data moves between devices by JAX's collectives and lax.ppermute only.
A program may use at most 64 MiB of HBM per device.

v0:
```python
import math

import jax
import jax.numpy as jnp
from jax import lax
from jax.sharding import PartitionSpec as P

R = 256
BINS = 32
NODES = 8


def split_gains(sums, tallies):
    left = jnp.cumsum(sums, axis=1)[:, :-1, :]
    whole = jnp.sum(sums, axis=1)
    left_count = jnp.cumsum(tallies, axis=1)[:, :-1]
    total = jnp.sum(tallies, axis=1)
    right_count = total[:, None] - left_count
    right = whole[:, None, :] - left
    differ = (
        left / jnp.maximum(left_count, 1.0)[:, :, None]
        - right / jnp.maximum(right_count, 1.0)[:, :, None]
    )
    factor = left_count * right_count / total[:, None]
    return factor * jnp.sum(differ * differ, axis=2)


def body(targets, omega, phase, codes, node, boot_counts):
    width_all = omega.shape[1]
    feat_dev = codes.shape[1]
    scaling = math.sqrt(2.0 / R)
    whole_targets = lax.all_gather(targets, "feat", axis=1, tiled=True)
    whole_omega = lax.all_gather(omega, "feat", axis=0, tiled=True)
    projected = lax.dot_general(
        whole_omega, whole_targets, (((0,), (1,)), ((), ())), preferred_element_type=jnp.float32
    )
    fourier = (scaling * jnp.cos(projected + phase[:, None])).astype(jnp.bfloat16)
    combined = (node[:, None] * BINS + codes).T
    weights_half = boot_counts.astype(jnp.bfloat16)
    slot_ids = jnp.arange(NODES * BINS, dtype=jnp.int32)

    def one_feature(column):
        table = jnp.where(
            column[None, :] == slot_ids[:, None], weights_half[None, :], jnp.zeros((), jnp.bfloat16)
        )
        sums = lax.dot_general(
            table, fourier, (((1,), (1,)), ((), ())), preferred_element_type=jnp.float32
        )
        tallies = jnp.sum(table, axis=1, dtype=jnp.float32)
        return (sums, tallies)

    histogram, tallies = lax.map(one_feature, combined)
    histogram = histogram.reshape(feat_dev * NODES, BINS, width_all)
    tallies = tallies.reshape(feat_dev * NODES, BINS)
    owned_count = feat_dev * NODES // lax.axis_size("rows")
    first_slot = lax.axis_index("rows") * owned_count
    summed, summed_tallies = lax.psum((histogram, tallies), "rows")
    mine = lax.dynamic_slice_in_dim(summed, first_slot, owned_count, 0)
    mine_tallies = lax.dynamic_slice_in_dim(summed_tallies, first_slot, owned_count, 0)
    gains = split_gains(mine, mine_tallies)
    node_of = (first_slot + jnp.arange(owned_count, dtype=jnp.int32)) % NODES
    slot_best = jnp.max(gains, axis=1)
    match = node_of[:, None] == jnp.arange(NODES, dtype=jnp.int32)[None, :]
    local_best = jnp.max(jnp.where(match, slot_best[:, None], 0.0), axis=0)
    best = lax.pmax(local_best, ("rows", "feat"))
    return (gains, best)


def solution(mesh):
    in_specs = (P("rows", "feat"), P("feat", None), P(), P("rows", "feat"), P("rows"), P("rows"))
    out_specs = (P(("feat", "rows"), None), P())
    return jax.shard_map(body, mesh=mesh, in_specs=in_specs, out_specs=out_specs, check_vma=False)
```

profile of v0, /device:TPU:0, one launch (start us, length us, event | category | flops | bytes accessed | tf_op | source)
XLA Modules:
  0.0 492.9 jit_solution(17544656276860813304)
XLA Ops:
  7.2 0.7 all-gather.2.cloned.1.call-update
  8.0 0.7 convert_element_type.9
  8.7 8.8 %all_gather.6 = bf16[1024,256]{1,0:T(8,128)(2,1)S(1)} all-gather(bf16[256,256]{1,0:T(8,128)(2,1)} %param.9), channel_id=1, replica_groups=mesh['rows'=8,'feat'=4] {'feat'}, dimensions={0}, use_global_device_ids=true | all-gather | bytes 655360 | tf_op jit(solution)/shard_map/all_gather | solution.py:33
  17.5 0.7 broadcast_multiply_fusion
  18.2 1.1 add_bitcast_fusion
  19.4 52.3 %all-gather.2.cloned.1.call-done = bf16[4096,1024]{1,0:T(8,128)(2,1)} async-done(((bf16[4096,256]{1,0:T(8,128)(2,1)}), bf16[4096,1024]{1,0:T(8,128)(2,1)}) %all-gather.2.cloned.1.call-update) | async-done | bytes 8388624 | tf_op jit(solution)/shard_map/all_gather | solution.py:32
  71.7 17.9 %fusion.17 = bf16[256,4096]{1,0:T(8,128)(2,1)S(1)} fusion(bf16[1024,256]{1,0:T(8,128)(2,1)S(1)} %all_gather.6, bf16[4096,1024]{1,0:T(8,128)(2,1)} %all-gather.2.cloned.1.call-done, f32[256]{0:T(256)} %param.10), kind=kOutput, calls=%fused_computation.15 | convolution fusion | flops 2150629376 | bytes 11011072 | tf_op jit(solution)/shard_map/dot_general | solution.py:34
  89.6 68.9 %while.13 = (s32[]{:T(128)}, f32[32,256,256]{2,1,0:T(8,128)}, f32[32,256]{1,0:T(8,128)S(1)}, s32[32,4096]{1,0:T(8,128)S(1)}, bf16[4096]{0:T(1024)(128)(2,1)S(1)}...) while((s32[]{:T(128)}, f32[32,256,256]{2,1,0:T(8,128)}, f32[32,256]{1,0:T(8,128)S(1)}, ...), condition=%wide.region_2.3_spmd.clone, body=%wide.region_0.2_spmd.clone.sunk | while | flops 543162112 | bytes 2444393 | solution.py:52
  89.6 0.6 convert_reduce_fusion.2
  90.3 1.4 fusion.35
  91.7 0.6 convert_reduce_fusion.2
  92.4 1.4 fusion.35
  93.9 0.6 convert_reduce_fusion.2
  94.6 1.5 fusion.35
  96.0 0.6 convert_reduce_fusion.2
  96.7 1.5 fusion.35
  98.9 1.5 fusion.35
  101.0 1.5 fusion.35
  103.2 1.5 fusion.35
  104.7 0.6 convert_reduce_fusion.2
  105.3 1.5 fusion.35
  107.5 1.5 fusion.35
  109.7 1.5 fusion.35
  111.8 1.5 fusion.35
  113.3 0.6 convert_reduce_fusion.2
  114.0 1.5 fusion.35
  115.4 0.6 convert_reduce_fusion.2
  116.1 1.5 fusion.35
  117.6 0.6 convert_reduce_fusion.2
  118.3 1.5 fusion.35
  120.4 1.4 fusion.35
  122.6 1.5 fusion.35
  124.1 0.6 convert_reduce_fusion.2
  124.7 1.4 fusion.35
  126.2 0.6 convert_reduce_fusion.2
  126.9 1.4 fusion.35
  129.0 1.5 fusion.35
  130.5 0.6 convert_reduce_fusion.2
  131.2 1.5 fusion.35
  132.7 0.6 convert_reduce_fusion.2
  133.3 1.5 fusion.35
  134.8 0.6 convert_reduce_fusion.2
  135.5 1.5 fusion.35
  137.7 1.5 fusion.35
  139.1 0.6 convert_reduce_fusion.2
  139.8 1.5 fusion.35
  141.3 0.6 convert_reduce_fusion.2
  142.0 1.5 fusion.35
  144.1 1.5 fusion.35
  146.3 1.5 fusion.35
  147.8 0.6 convert_reduce_fusion.2
  148.4 1.5 fusion.35
  150.6 1.4 fusion.35
  152.1 0.6 convert_reduce_fusion.2
  152.7 1.4 fusion.35
  154.9 1.4 fusion.35
  157.0 1.5 fusion.35
  158.5 11.4 %copy.18 = f32[256,32,256]{2,0,1:T(8,128)} copy(f32[256,32,256]{2,1,0:T(8,128)} %bitcast.20) | data formatting | bytes 16777216 | tf_op jit(solution)/shard_map/reshape | solution.py:53
  170.1 42.1 %psum.14 = f32[256,32]{1,0:T(8,128)S(1)} all-reduce(f32[256,32]{1,0:T(8,128)S(1)} %reshape.35), channel_id=1, replica_groups=mesh['rows'=8,'feat'=4] {'rows'}, use_global_device_ids=true, to_apply=%region_3.4 | all-reduce | flops 8192 | bytes 65536 | tf_op jit(solution)/shard_map/psum | solution.py:57
  212.8 229.9 %all-reduce.2.cloned.1.call-done = f32[256,32,256]{2,0,1:T(8,128)} async-done(((f32[256,32,256]{2,0,1:T(8,128)}), f32[256,32,256]{2,0,1:T(8,128)}) %all-reduce.2.cloned.1.call-update) | async-done | bytes 8388624 | tf_op jit(solution)/shard_map/psum | solution.py:57
  442.6 1.3 dynamic-slice_reduce_fusion
  443.9 1.3 fusion.18
  445.8 0.8 fusion.24
  446.7 39.3 %pmax.7 = f32[8]{0:T(128)} all-reduce(f32[8]{0:T(128)S(1)} %select_reduce_fusion), channel_id=1, replica_groups=mesh['rows'=8,'feat'=4] {'rows','feat'}, use_global_device_ids=true, to_apply=%region_12.13 | all-reduce | flops 8 | bytes 64 | tf_op jit(solution)/shard_map/pmax | solution.py:65
  (94 shorter events, 12.6 us)
Async XLA Ops:
  7.2 64.5 %all-gather.2.cloned.1.call-start = ((), (), s32[]{:S(2)}) async-start(), calls=%async_computation | async-start | bytes 10485760 | tf_op jit(solution)/shard_map/all_gather | solution.py:32
  7.9 434.7 %all-reduce.2.cloned.1.call-start = ((), (), s32[]{:S(2)}) async-start(), calls=%async_computation.1 | async-start | bytes 16777216 | tf_op jit(solution)/shard_map/psum | solution.py:57
Sparse Core Ops, SparseCore 0:
  9.5 62.0 all-gather.1
  170.1 272.5 all-reduce.1
where the time goes:
time: 493 us
  waiting for transfers between devices  283 us (57%)
  blocking collectives  90.3 us (18%)
  matrix products  64.5 us (13%)
  other arithmetic  27.3 us (6%)
  between operations  14.1 us (3%)
  local copies, waits for them, and re-layouts  13.5 us (3%)
    psum x1, waiting for transfers between devices, body(): summed, summed_tallies = lax.psum((histogram, tallies), 'rows')  230 us
    all_gather x1, waiting for transfers between devices, body(): whole_targets = lax.all_gather(targets, 'feat', axis=1, tiled=True)  52.3 us
    dot_general x32, matrix products, one_feature(): lax.dot_general(table, fourier, (((1,), (1,)), ((), ())), preferred_eleme...  46.6 us
    psum x1, blocking collectives, body(): summed, summed_tallies = lax.psum((histogram, tallies), 'rows')  42.1 us
    pmax x1, blocking collectives, body(): best = lax.pmax(local_best, ('rows', 'feat'))  39.3 us
    reduce_sum x32, other arithmetic, one_feature(): tallies = jnp.sum(table, axis=1, dtype=jnp.float32)  20.3 us
    dot_general x1, matrix products, body(): lax.dot_general(whole_omega, whole_targets, (((0,), (1,)), ((), ())), pre...  17.9 us
    reshape x1, local copies, waits for them, and re-layouts, body(): histogram = histogram.reshape(feat_dev * NODES, BINS, width_all)  11.4 us
  transfers between devices with their start and end apart: 2, of which 2 were waited for; matrix products, arithmetic and copies ran while one was open for 1% of the time, Pallas kernels for 0%

commit v1 on v0

v1 whole, which is shorter than its diff:
```python
import functools
import math

import jax
import jax.numpy as jnp
from jax import lax
from jax.experimental import pallas as pl
from jax.experimental.pallas import tpu as pltpu
from jax.sharding import PartitionSpec as P

BINS = 32
NODES = 8
LANES = 128
EXTRA = 16
STEPS = 65536.0
PARAMS = pltpu.CompilerParams(vmem_limit_bytes=40 * 1024 * 1024)
VMEM = pl.BlockSpec(memory_space=pltpu.VMEM)
SMEM = pl.BlockSpec(memory_space=pltpu.SMEM)


def rank_kernel(room, node_ref, boot_ref, pos_ref, rounds_ref):
    node = node_ref[...]
    live = boot_ref[...] > 0
    groups = node.shape[0]
    block = groups * LANES
    members = [jnp.where((node == n) & live, 1.0, 0.0) for n in range(NODES)]
    member = jnp.concatenate(members, axis=0)
    size = NODES * groups
    i = lax.broadcasted_iota(jnp.int32, (LANES, LANES), 0)
    j = lax.broadcasted_iota(jnp.int32, (LANES, LANES), 1)
    before = jnp.where(i < j, 1.0, 0.0).astype(jnp.bfloat16)
    inside = jnp.dot(member.astype(jnp.bfloat16), before, preferred_element_type=jnp.float32)
    count = jnp.sum(member, axis=1, keepdims=True)
    p = lax.broadcasted_iota(jnp.int32, (size, size), 0)
    q = lax.broadcasted_iota(jnp.int32, (size, size), 1)
    earlier = jnp.where((p // groups == q // groups) & (q < p), 1.0, 0.0).astype(jnp.bfloat16)
    spread = jnp.broadcast_to(count, (size, LANES))
    base = jnp.dot(earlier, spread.astype(jnp.bfloat16), preferred_element_type=jnp.float32)
    rank = inside + base
    pos = jnp.zeros((groups, LANES), jnp.float32)
    for n in range(NODES):
        pos += members[n] * (rank[n * groups : (n + 1) * groups] + float(n * block))
    pos_ref[...] = jnp.where(live, pos, -1.0).astype(jnp.int32)
    most = jnp.max(base + spread).astype(jnp.int32)
    rounds_ref[0] = (most + (room - 1)) // room


def sort_kernel(distance, slots, room, last, where_ref, pos_ref, t0_ref, t1_ref, o0_ref, o1_ref, codes_ref, out_ref, sorted_ref, pick):
    groups = pos_ref.shape[0]
    block = groups * LANES
    x, a, turn, rounds = where_ref[0], where_ref[1], where_ref[2], where_ref[3]
    for slot in range(slots):
        node = (x ^ distance) * slots + (a ^ slot)
        start = node * block + turn * room
        wanted = start + lax.broadcasted_iota(jnp.int32, (room, LANES), 0)
        for g in range(groups):
            pick[slot * room : (slot + 1) * room, g * LANES : (g + 1) * LANES] = jnp.where(
                pos_ref[g : g + 1, :] == wanted, 1.0, 0.0
            ).astype(jnp.bfloat16)
    s0 = jnp.dot(pick[...], t0_ref[...], preferred_element_type=jnp.float32).astype(jnp.bfloat16)
    s1 = jnp.dot(pick[...], t1_ref[...], preferred_element_type=jnp.float32).astype(jnp.bfloat16)
    partial = jnp.dot(s0, o0_ref[...], preferred_element_type=jnp.float32)
    partial += jnp.dot(s1, o1_ref[...], preferred_element_type=jnp.float32)
    turns = partial * (0.5 / math.pi)
    turns = turns - jnp.floor(turns)
    if distance:
        coded = jnp.minimum((turns * STEPS).astype(jnp.int32), 65535) - 32768
        out_ref[...] = coded.astype(jnp.int16)
    else:
        out_ref[...] = turns
    moved = lax.dot_general(
        codes_ref[...], pick[...], (((1,), (1,)), ((), ())), preferred_element_type=jnp.float32
    )
    line = lax.broadcasted_iota(jnp.int32, moved.shape, 0)
    moved = jnp.where(line == last, rounds.astype(jnp.float32), moved)
    sorted_ref[...] = moved.astype(jnp.bfloat16)


def cosine_kernel(slots, own_ref, phase_ref, *refs):
    received, outs = refs[:-slots], refs[-slots:]
    width = phase_ref.shape[1]
    room = outs[0].shape[0]
    scaling = math.sqrt(2.0 / width)
    series = [(-1.0) ** (k + 1) * (2 * math.pi) ** (2 * k + 1) / math.factorial(2 * k + 1) for k in range(7)]
    shift = phase_ref[...] * (0.5 / math.pi)
    for slot in range(slots):
        rows = pl.ds(slot * room, room)
        turns = own_ref[rows, :] + shift
        for ref in received:
            turns += (ref[rows, :].astype(jnp.float32) + 32768.5) * (1.0 / STEPS)
        turns = jnp.abs(turns - jnp.floor(turns + 0.5)) - 0.25
        square = turns * turns
        value = jnp.full_like(turns, series[-1])
        for term in series[-2::-1]:
            value = value * square + term
        outs[slot][...] = (scaling * (value * turns)).astype(jnp.bfloat16)


def gains_of(left, counts):
    whole = left[..., BINS - 1 :, :]
    total = counts[..., BINS - 1 :, :]
    other = total - counts
    differ = left * (1.0 / jnp.maximum(counts, 1.0)) - (whole - left) * (1.0 / jnp.maximum(other, 1.0))
    return (counts * other / total) * jnp.sum(differ * differ, axis=-1, keepdims=True)


def histogram_kernel(features, codes_ref, *refs):
    *pieces, left_ref, counts_ref, gains_ref, table = refs
    length = pieces[0].shape[0]
    slots = features * BINS
    threshold = lax.broadcasted_iota(jnp.int32, (BINS, length), 0).astype(jnp.float32)
    for index, piece in enumerate(pieces):
        span = slice(index * length, (index + 1) * length)
        codes = codes_ref[:, span].astype(jnp.float32)
        weight = codes[features : features + 1, :]
        for f in range(features):
            rows = slice(f * BINS, (f + 1) * BINS)
            entry = jnp.where(codes[f : f + 1, :] <= threshold, weight, 0.0)
            table[rows, :] = entry.astype(jnp.bfloat16)
            folded = entry[:, :LANES]
            for g in range(1, length // LANES):
                folded += entry[:, g * LANES : (g + 1) * LANES]
            if index:
                folded += counts_ref[rows, :]
            counts_ref[rows, :] = folded
        sums = jnp.dot(table[...], piece[...], preferred_element_type=jnp.float32)
        if index:
            left_ref[...] += sums
        else:
            left_ref[...] = sums
    per_line = LANES // BINS
    i = lax.broadcasted_iota(jnp.int32, (LANES, LANES), 0)
    j = lax.broadcasted_iota(jnp.int32, (LANES, LANES), 1)
    for line in range(slots // LANES):
        columns = []
        for f in range(line * per_line, (line + 1) * per_line):
            rows = slice(f * BINS, (f + 1) * BINS)
            counts = jnp.sum(counts_ref[rows, :], axis=1, keepdims=True)
            columns.append(gains_of(left_ref[rows, :], counts))
        column = jnp.concatenate(columns, axis=0)
        gains_ref[line : line + 1, :] = jnp.sum(jnp.where(i == j, column, 0.0), axis=0, keepdims=True)


def split_rows(mesh_sizes, targets, omega, phase, codes, node, boot_counts):
    groups_all, feat_all = mesh_sizes
    chips = feat_all // 2
    slots = NODES // chips
    copies = groups_all // slots
    rows_dev, feat_dev = codes.shape
    width = omega.shape[1]
    block = rows_dev // 2
    room = block // NODES
    owned = feat_dev * NODES // groups_all
    per_owner = max(1, owned // NODES)
    sets = feat_dev // per_owner
    lines = sets // copies
    part = lines * per_owner
    features = chips * part

    feat, place = lax.axis_index("feat"), lax.axis_index("rows")
    x, core = feat // 2, feat % 2
    major, minor = place // copies, place % copies

    def permute(axis, size, distance, array):
        return lax.ppermute(array, axis, [(i, i ^ distance) for i in range(size)])

    swap = functools.partial(permute, "feat", feat_all, 1)

    def along_x(distance, array):
        return permute("feat", feat_all, 2 * distance, array)

    def along_major(distance, array):
        return permute("rows", groups_all, copies * distance, array)

    def along_minor(distance, array):
        return permute("rows", groups_all, distance, array)

    mine, theirs = core * block, (1 - core) * block
    targets_theirs = swap(lax.dynamic_slice_in_dim(targets, theirs, block, 0))
    targets_mine = lax.dynamic_slice_in_dim(targets, mine, block, 0)
    omega_theirs = swap(omega)

    half = codes.astype(jnp.bfloat16).T.reshape(lines, copies, per_owner, rows_dev)
    half = jnp.concatenate([lax.dynamic_slice_in_dim(half, minor ^ d, 1, 1) for d in range(copies)], axis=1)
    half = half.transpose(1, 0, 2, 3).reshape(feat_dev, rows_dev)
    half_mine = lax.dynamic_slice_in_dim(half, mine, block, 1)
    half_theirs = swap(lax.dynamic_slice_in_dim(half, theirs, block, 1))
    node_mine = lax.dynamic_slice_in_dim(node, mine, block, 0).reshape(block // LANES, LANES)
    boot_mine = lax.dynamic_slice_in_dim(boot_counts, mine, block, 0).reshape(block // LANES, LANES)
    weights = boot_mine.astype(jnp.bfloat16).reshape(1, block)
    extra = jnp.concatenate([weights, jnp.zeros((EXTRA - 1, block), jnp.bfloat16)], axis=0)
    table = jnp.concatenate([half_mine, half_theirs, extra], axis=0)
    both = 2 * feat_dev

    pos, rounds = pl.pallas_call(
        functools.partial(rank_kernel, room),
        out_shape=(
            jax.ShapeDtypeStruct((block // LANES, LANES), jnp.int32),
            jax.ShapeDtypeStruct((1,), jnp.int32),
        ),
        in_specs=[VMEM, VMEM],
        out_specs=(VMEM, SMEM),
        compiler_params=PARAMS,
        name="rank",
    )(node_mine, boot_mine)

    def sort(distance, turn):
        return pl.pallas_call(
            functools.partial(sort_kernel, distance, slots, room, both + 1),
            out_shape=(
                jax.ShapeDtypeStruct((slots * room, width), jnp.int16 if distance else jnp.float32),
                jax.ShapeDtypeStruct((both + EXTRA, slots * room), jnp.bfloat16),
            ),
            in_specs=[SMEM] + [VMEM] * 6,
            out_specs=(VMEM, VMEM),
            scratch_shapes=[pltpu.VMEM((slots * room, block), jnp.bfloat16)],
            compiler_params=PARAMS,
            cost_estimate=pl.CostEstimate(
                flops=2 * slots * room * block * (2 * targets.shape[1] + both), bytes_accessed=4 << 20, transcendentals=0
            ),
            name="sort",
        )(
            jnp.stack([x, major, turn, rounds[0]]).astype(jnp.int32),
            pos, targets_mine, targets_theirs, omega, omega_theirs, table,
        )

    def one_round(turn):
        sent = [sort(d, turn) for d in range(1, chips)]
        angles = [along_x(d, sent[d - 1][0]) for d in range(1, chips)]
        own_angles, own_codes = sort(0, turn)
        chip_codes = [own_codes] + [along_x(d, sent[d - 1][1][:both]) for d in range(1, chips)]
        chip_codes = jnp.concatenate(chip_codes, axis=0)
        arrived = []
        for d in range(slots):
            piece = chip_codes[:, d * room : (d + 1) * room]
            arrived.append(along_major(d, piece) if d else piece)
        node_codes = jnp.concatenate(arrived, axis=1)
        span = slots * room

        fourier = pl.pallas_call(
            functools.partial(cosine_kernel, slots),
            out_shape=tuple(jax.ShapeDtypeStruct((room, width), jnp.bfloat16) for _ in range(slots)),
            in_specs=[VMEM] * (chips + 1),
            out_specs=tuple(VMEM for _ in range(slots)),
            compiler_params=PARAMS,
            cost_estimate=pl.CostEstimate(flops=30 * span * width, bytes_accessed=2 << 20, transcendentals=0),
            name="cosine",
        )(own_angles, phase.reshape(1, width), *angles)
        fourier = jnp.concatenate([along_major(d, fourier[d]) if d else fourier[d] for d in range(slots)], axis=0)

        first, rest = node_codes[:both], node_codes[both + EXTRA :]
        extras = node_codes[both : both + EXTRA]
        by_part = jnp.concatenate([first, rest], axis=0).reshape(chips, 2, copies, part, span)
        held = []
        for d in range(copies):
            piece = jnp.concatenate([by_part[:, :, d].reshape(chips * 2 * part, span), extras], axis=0)
            held.append(along_minor(d, piece) if d else piece)
        held = jnp.concatenate(held, axis=1)
        by_core = held[: 2 * features].reshape(chips, 2, part, copies * span)
        keep = jnp.concatenate([by_core[:, 0].reshape(features, copies * span), held[2 * features :]], axis=0)
        give = jnp.concatenate([by_core[:, 1].reshape(features, copies * span), held[2 * features :]], axis=0)
        final_codes = jnp.concatenate([keep, swap(give)], axis=1)

        pieces = [along_minor(d, fourier) if d else fourier for d in range(copies)]
        pieces = pieces + [swap(piece) for piece in pieces]
        left, counts, gains = pl.pallas_call(
            functools.partial(histogram_kernel, features),
            out_shape=(
                jax.ShapeDtypeStruct((features * BINS, width), jnp.float32),
                jax.ShapeDtypeStruct((features * BINS, LANES), jnp.float32),
                jax.ShapeDtypeStruct((features * BINS // LANES, LANES), jnp.float32),
            ),
            in_specs=[VMEM] * (1 + len(pieces)),
            out_specs=(VMEM, VMEM, VMEM),
            scratch_shapes=[pltpu.VMEM((features * BINS, span), jnp.bfloat16)],
            compiler_params=PARAMS,
            name="histogram",
        )(final_codes, *pieces)
        return left, counts, gains, final_codes[features + 1]

    left, counts, gains, flags = one_round(jnp.int32(0))
    needed = jnp.max(flags.astype(jnp.float32)).astype(jnp.int32)

    def more_rounds():
        def step(state):
            turn, left, counts = state
            more_left, more_counts, _, _ = one_round(turn)
            return turn + 1, left + more_left, counts + more_counts

        _, all_left, all_counts = lax.while_loop(lambda state: state[0] < needed, step, (jnp.int32(1), left, counts))
        tallies = jnp.sum(all_counts, axis=1).reshape(features, BINS, 1)
        return gains_of(all_left.reshape(features, BINS, width), tallies).reshape(gains.shape)

    gains = lax.cond(needed > 1, more_rounds, lambda: gains)
    gains = gains.reshape(chips, lines, per_owner, BINS)
    largest = jnp.max(gains[..., : BINS - 1])
    gains = lax.switch(x, [functools.partial(lambda g, o: jnp.stack([g[i ^ o] for i in range(chips)]), gains, o) for o in range(chips)])

    line_of = [(i // (groups_all // sets)) // copies for i in range(groups_all)]
    load = per_owner * BINS
    send = jnp.stack([gains[:, line].reshape(chips, 1, load) for line in line_of])
    send = jnp.broadcast_to(send, (groups_all, chips, 2, load))
    top = jnp.full((groups_all, chips, 2, load), largest)
    send = jnp.stack([send, top], axis=3).reshape(groups_all * feat_all, 2, load)
    got = lax.all_to_all(send, ("rows", "feat"), 0, 0).reshape(slots, copies, chips, 2, 2, load)
    best = jnp.max(got[:, :, :, :, 1, 0], axis=(1, 3)).T.reshape(NODES)
    source = (place // (groups_all // sets)) % copies
    took = lax.dynamic_slice_in_dim(got[:, :, :, :, 0], source, 1, 1)
    took = lax.dynamic_slice_in_dim(took, core, 1, 3)
    took = took.reshape(slots, chips, per_owner, BINS).transpose(2, 1, 0, 3).reshape(per_owner * NODES, BINS)
    took = lax.dynamic_slice_in_dim(took, (place * owned) % (per_owner * NODES), owned, 0)
    return took[:, : BINS - 1], best


def solution(mesh):
    in_specs = (P("rows", "feat"), P("feat", None), P(), P("rows", "feat"), P("rows"), P("rows"))
    out_specs = (P(("feat", "rows"), None), P())
    sizes = (mesh.shape["rows"], mesh.shape["feat"])
    return jax.shard_map(
        functools.partial(split_rows, sizes), mesh=mesh, in_specs=in_specs, out_specs=out_specs, check_vma=False
    )
```

time: 493 us -> 87.2 us (0.18)
  waiting for transfers between devices: 283 us -> 35.3 us
  blocking collectives: 90.3 us -> 0 us
  matrix products: 64.5 us -> 0 us
  other arithmetic: 27.3 us -> 2.45 us
  starting transfers between devices: 0.08 us -> 22.8 us
  Pallas kernels: 0 us -> 17 us
  between operations: 14.1 us -> 1.79 us
  local copies, waits for them, and re-layouts: 13.5 us -> 7.51 us
    psum x1 -> x0, waiting for transfers between devices: 230 us -> none  [body(): summed, summed_tallies = lax.psum((histogram, tallies), 'rows')]
    dot_general x33 -> x0, matrix products: 64.5 us -> none  [the longest x32 46.6 us: one_feature(): lax.dot_general(table, fourier, (((1,), (1,)), ((), ())), preferred_eleme...]
    all_gather x1 -> x0, waiting for transfers between devices: 52.3 us -> none  [body(): whole_targets = lax.all_gather(targets, 'feat', axis=1, tiled=True)]
    psum x1 -> x0, blocking collectives: 42.1 us -> none  [body(): summed, summed_tallies = lax.psum((histogram, tallies), 'rows')]
    pmax x1 -> x0, blocking collectives: 39.3 us -> none  [body(): best = lax.pmax(local_best, ('rows', 'feat'))]
    ppermute x0 -> x16, waiting for transfers between devices: none -> 28 us  [permute(): return lax.ppermute(array, axis, [(i, i ^ distance) for i in range(size)])]
    reduce_sum x35 -> x0, other arithmetic: 22.2 us -> none  [the longest x32 20.3 us: one_feature(): tallies = jnp.sum(table, axis=1, dtype=jnp.float32)]
    pallas_call x0 -> x5, Pallas kernels: none -> 17 us  [the longest x2 11 us: sort(): pl.pallas_call(functools.partial(sort_kernel, distance, slots, room, both...]
  transfers between devices with their start and end apart: 2 -> 17, of which waited for: 2 -> 8; matrix products, arithmetic and copies ran while one was open for 1% -> 3% of each run, Pallas kernels for 0% -> 7%
where the time goes in v1:
time: 87.2 us; the launch traced here: 86.8 us
  waiting for transfers between devices  35.3 us (40%)
  starting transfers between devices  22.8 us (26%)
  Pallas kernels  17 us (19%)
  local copies, waits for them, and re-layouts  7.51 us (9%)
  other arithmetic  2.45 us (3%)
  between operations  1.79 us (2%)
    ppermute x16, waiting for transfers between devices, permute(): return lax.ppermute(array, axis, [(i, i ^ distance) for i in range(size)])  28 us
    ppermute x16, starting transfers between devices, permute(): return lax.ppermute(array, axis, [(i, i ^ distance) for i in range(size)])  16.9 us
    pallas_call x2, Pallas kernels, sort(): pl.pallas_call(functools.partial(sort_kernel, distance, slots, room, both...  11 us
    all_to_all x1, waiting for transfers between devices, split_rows(): lax.all_to_all(send, ('rows', 'feat'), 0, 0)  7.23 us
    all_to_all x1, starting transfers between devices, split_rows(): lax.all_to_all(send, ('rows', 'feat'), 0, 0)  5.92 us
    pallas_call x1, Pallas kernels, one_round(): pl.pallas_call(functools.partial(histogram_kernel, features), out_shape=(...  4.19 us
  transfers between devices with their start and end apart: 17, of which 8 were waited for; matrix products, arithmetic and copies ran while one was open for 3% of the time, Pallas kernels for 7%

profile of v1, /device:TPU:0, one launch (start us, length us, event | category | flops | bytes accessed | tf_op | source)
XLA Modules:
  0.0 86.8 jit_solution(4650920413676846143)
XLA Ops:
  0.6 0.0 copy-start
  0.7 1.7 %constant_dynamic-slice_fusion.2 = (bf16[2048,256]{1,0:T(8,128)(2,1)S(1)}, bf16[2048,256]{1,0:T(8,128)(2,1)S(1)}) fusion(bf16[4096,256]{1,0:T(8,128)(2,1)} %param.12, s32[]{:T(128)S(6)} %select_n.52, s32[]{:T(128)S(6)} %select_n.51), kind=kLoop, calls=%fused_computation.64 | loop fusion | bytes 4194312 | tf_op jit(solution)/shard_map/dynamic_slice | solution.py:179
  2.4 0.0 copy-start.11
  2.4 0.0 copy-start.10
  2.5 0.5 collective-permute-start.13
  3.0 0.1 reshape.149
  3.1 0.1 dynamic-slice_bitcast_fusion.1
  3.2 0.2 maximum_bitcast_fusion
  3.4 0.1 reshape.150
  3.5 0.1 collective-permute-start.15
  3.7 0.5 collective-permute-start.14
  4.2 0.1 pad.42.clone
  4.3 0.9 %rank.1 = (s32[16,128]{1,0:T(8,128)S(1)}, s32[1]{0:T(128)}) custom-call(s32[16,128]{1,0:T(8,128)S(1)} %dynamic-slice_bitcast_fusion.2.node_ref, s32[16,128]{1,0:T(8,128)S(1)} %get-tuple-element.267.boot_ref), custom_call_target="tpu_custom_call" | custom-call | tf_op jit(solution)/shard_map/rank/pallas_call | solution.py:195
  5.2 0.6 pad_add_fusion.1.where_ref
  5.8 0.0 collective-permute-done.15
  5.8 0.1 maximum_maximum_fusion.codes_ref
  5.9 0.0 collective-permute-done.14.o1_ref
  6.0 0.0 collective-permute-done.13.t1_ref
  6.0 5.6 %sort.5 = (s16[1024,256]{1,0:T(8,128)(2,1)S(1)}, bf16[80,1024]{1,0:T(8,128)(2,1)S(1)}) custom-call(s32[4]{0:T(128)S(1)} %pad_add_fusion.1.where_ref, s32[16,128]{1,0:T(8,128)S(1)} %get-tuple-element.188.pos_ref, bf16[2048,256]{1,0:T(8,128)(2,1)S(1)} %get-tuple-element.247.t0_ref, bf16[2048,256]{1,0:T(8,128)(2,1)} %collective-permute-done.13.t1_ref, ...), custom_call_target="tpu_custom_call" | custom-call | flops 2415919104 | bytes 4194304 | tf_op jit(solution)/shard_map/sort/pallas_call | solution.py:208
  11.6 2.6 %collective-permute-start.16 = (bf16[64,1024]{1,0:T(8,128)(2,1)S(1)}, bf16[64,1024]{1,0:T(8,128)(2,1)S(1)}, u32[]{:S(2)}, u32[]{:S(2)}) collective-permute-start(bf16[64,1024]{1,0:T(8,128)(2,1)S(1)} %slice.176), channel_id=1, source_target_pairs={{0,2},{1,3},{2,0},{3,1},{4,6},{5,7},{6,4},{7,5},{8,10},{9,11},{10,... | collective-permute-start | bytes 393224 | tf_op jit(solution)/shard_map/ppermute | solution.py:165
  14.3 5.4 %sort.4 = (f32[1024,256]{1,0:T(8,128)S(1)}, bf16[80,1024]{1,0:T(8,128)(2,1)S(1)}) custom-call(s32[4]{0:T(128)S(1)} %pad_add_fusion.1.where_ref, s32[16,128]{1,0:T(8,128)S(1)} %get-tuple-element.188.pos_ref, bf16[2048,256]{1,0:T(8,128)(2,1)S(1)} %get-tuple-element.247.t0_ref, bf16[2048,256]{1,0:T(8,128)(2,1)} %collective-permute-done.13.t1_ref, ...), custom_call_target="tpu_custom_call" | custom-call | flops 2415919104 | bytes 4194304 | tf_op jit(solution)/shard_map/sort/pallas_call | solution.py:208
  19.7 0.0 collective-permute-done.16
  19.8 0.0 copy-start.8
  19.8 1.6 %collective-permute-start.17 = (bf16[144,256]{1,0:T(8,128)(2,1)S(1)}, bf16[144,256]{1,0:T(8,128)(2,1)S(1)}, u32[]{:S(2)}, u32[]{:S(2)}) collective-permute-start(bf16[144,256]{1,0:T(8,128)(2,1)S(1)} %get-tuple-element.253), channel_id=1, source_target_pairs={{0,8},{4,12},{8,0},{12,4},{16,24},{20,28},{24,16},{28,20},{1,9},{5... | collective-permute-start | bytes 221192 | tf_op jit(solution)/shard_map/ppermute | solution.py:165
  21.4 2.6 %collective-permute-start.18 = (bf16[144,256]{1,0:T(8,128)(2,1)S(1)}, bf16[144,256]{1,0:T(8,128)(2,1)S(1)}, u32[]{:S(2)}, u32[]{:S(2)}) collective-permute-start(bf16[144,256]{1,0:T(8,128)(2,1)S(1)} %get-tuple-element.252), channel_id=1, source_target_pairs={{0,16},{4,20},{8,24},{12,28},{16,0},{20,4},{24,8},{28,12},{1,17},{... | collective-permute-start | bytes 221192 | tf_op jit(solution)/shard_map/ppermute | solution.py:165
  24.0 0.2 collective-permute-start.19
  24.2 0.4 collective-permute-start.22
  24.6 0.0 collective-permute-done.17
  24.6 5.7 %collective-permute-done.18 = bf16[144,256]{1,0:T(8,128)(2,1)S(1)} collective-permute-done((bf16[144,256]{1,0:T(8,128)(2,1)S(1)}, bf16[144,256]{1,0:T(8,128)(2,1)S(1)}, u32[]{:S(2)}, u32[]{:S(2)}) %collective-permute-start.18) | collective-permute-done | bytes 73760 | tf_op jit(solution)/shard_map/ppermute | solution.py:165
  30.3 0.0 collective-permute-done.19
  30.4 1.6 %collective-permute-start.20 = (bf16[80,1024]{1,0:T(8,128)(2,1)S(1)}, bf16[80,1024]{1,0:T(8,128)(2,1)S(1)}, u32[]{:S(2)}, u32[]{:S(2)}) collective-permute-start(bf16[80,1024]{1,0:T(8,128)(2,1)S(1)} %pad_maximum_fusion.14), channel_id=1, source_target_pairs={{0,4},{4,0},{8,12},{12,8},{16,20},{20,16},{24,28},{28,24},{1,5},{5... | collective-permute-start | bytes 491528 | tf_op jit(solution)/shard_map/ppermute | solution.py:165
  32.0 3.8 %collective-permute-done.20 = bf16[80,1024]{1,0:T(8,128)(2,1)S(1)} collective-permute-done((bf16[80,1024]{1,0:T(8,128)(2,1)S(1)}, bf16[80,1024]{1,0:T(8,128)(2,1)S(1)}, u32[]{:S(2)}, u32[]{:S(2)}) %collective-permute-start.20) | collective-permute-done | bytes 163872 | tf_op jit(solution)/shard_map/ppermute | solution.py:165
  35.9 1.6 %collective-permute-done.22.refs_0_ = s16[1024,256]{1,0:T(8,128)(2,1)S(1)} collective-permute-done((s16[1024,256]{1,0:T(8,128)(2,1)S(1)}, s16[1024,256]{1,0:T(8,128)(2,1)S(1)}, u32[]{:S(2)}, u32[]{:S(2)}) %collective-permute-start.22) | collective-permute-done | bytes 524320 | tf_op jit(solution)/shard_map/ppermute | solution.py:165
  37.5 0.9 %cosine.2 = (bf16[256,256]{1,0:T(8,128)(2,1)S(1)}, bf16[256,256]{1,0:T(8,128)(2,1)S(1)}, bf16[256,256]{1,0:T(8,128)(2,1)S(1)}, bf16[256,256]{1,0:T(8,128)(2,1)S(1)}) custom-call(f32[1024,256]{1,0:T(8,128)S(1)} %get-tuple-element.191.own_ref, f32[1,256]{1,0:T(1,128)S(1)} %bitcast.95, s16[1024,256]{1,0:T(8,128)(2,1)S(1)} %collective-permute-done.22.refs_0_), custom_call_target="tpu_custom_call" | custom-call | flops 7864320 | bytes 2097152 | tf_op jit(solution)/shard_map/cosine/pallas_call | solution.py:240
  38.4 0.7 collective-permute-start.23
  39.1 3.6 %collective-permute-start.24 = (bf16[256,256]{1,0:T(8,128)(2,1)S(1)}, bf16[256,256]{1,0:T(8,128)(2,1)S(1)}, u32[]{:S(2)}, u32[]{:S(2)}) collective-permute-start(bf16[256,256]{1,0:T(8,128)(2,1)S(1)} %get-tuple-element.195), channel_id=1, source_target_pairs={{0,16},{4,20},{8,24},{12,28},{16,0},{20,4},{24,8},{28,12},{1,17},{... | collective-permute-start | bytes 393224 | tf_op jit(solution)/shard_map/ppermute | solution.py:165
  42.6 0.3 collective-permute-start.25
  43.0 1.5 %collective-permute-done.23 = bf16[256,256]{1,0:T(8,128)(2,1)S(1)} collective-permute-done((bf16[256,256]{1,0:T(8,128)(2,1)S(1)}, bf16[256,256]{1,0:T(8,128)(2,1)S(1)}, u32[]{:S(2)}, u32[]{:S(2)}) %collective-permute-start.23) | collective-permute-done | bytes 131104 | tf_op jit(solution)/shard_map/ppermute | solution.py:165
  44.5 7.0 %collective-permute-done.24 = bf16[256,256]{1,0:T(8,128)(2,1)S(1)} collective-permute-done((bf16[256,256]{1,0:T(8,128)(2,1)S(1)}, bf16[256,256]{1,0:T(8,128)(2,1)S(1)}, u32[]{:S(2)}, u32[]{:S(2)}) %collective-permute-start.24) | collective-permute-done | bytes 131104 | tf_op jit(solution)/shard_map/ppermute | solution.py:165
  51.4 0.0 collective-permute-done.25
  51.5 1.6 %collective-permute-start.26 = (bf16[1024,256]{1,0:T(8,128)(2,1)S(1)}, bf16[1024,256]{1,0:T(8,128)(2,1)S(1)}, u32[]{:S(2)}, u32[]{:S(2)}) collective-permute-start(bf16[1024,256]{1,0:T(8,128)(2,1)S(1)} %constant_dynamic-update-slice_fusion.8.refs_0_), channel_id=1, source_target_pairs={{0,4},{4,0},{8,12},{12,8},{16,20},{20,16},{24,28},{28,24},{1,5},{5... | collective-permute-start | bytes 1572872 | tf_op jit(solution)/shard_map/ppermute | solution.py:165
  53.1 0.1 collective-permute-start.21
  53.2 0.5 collective-permute-start.27
  53.7 8.0 %collective-permute-done.26.refs_1_ = bf16[1024,256]{1,0:T(8,128)(2,1)S(1)} collective-permute-done((bf16[1024,256]{1,0:T(8,128)(2,1)S(1)}, bf16[1024,256]{1,0:T(8,128)(2,1)S(1)}, u32[]{:S(2)}, u32[]{:S(2)}) %collective-permute-start.26) | collective-permute-done | bytes 524320 | tf_op jit(solution)/shard_map/ppermute | solution.py:165
  61.6 0.0 collective-permute-start.28
  61.7 0.6 slice_reduce_fusion.2
  63.0 0.6 collective-permute-done.28.refs_3_
  63.5 4.2 %histogram.2 = (f32[1024,256]{1,0:T(8,128)S(1)}, f32[1024,128]{1,0:T(8,128)}, f32[8,128]{1,0:T(8,128)}) custom-call(bf16[48,4096]{1,0:T(8,128)(2,1)S(1)} %pad_maximum_fusion.9.codes_ref, bf16[1024,256]{1,0:T(8,128)(2,1)S(1)} %constant_dynamic-update-slice_fusion.8.refs_0_, bf16[1024,256]{1,0:T(8,128)(2,1)S(1)} %collective-permute-done.26.refs_1_, ...), custom_call_target="tpu_custom_call" | custom-call | tf_op jit(solution)/shard_map/histogram/pallas_call | solution.py:266
  67.7 2.1 %conditional.2 = (f32[2,4,4,32]{3,2,1,0:T(4,128)}, f32[2,4,4,32]{3,2,1,0:T(4,128)S(1)}) conditional(s32[]{:T(128)} %convert_element_type.21, f32[8,128]{1,0:T(8,128)} %get-tuple-element.197, (s32[]{:T(128)}, s32[]{:T(128)}, s32[]{:T(128)}, s32[1]{0:T(128)}, s32[16,128]{1,0:T(8,128)}, /*index=5*/bf16[2048,256]{1,0:T(8,128)(2,1)}, ...), branch_computations={%region_1.2_spmd, %region_2.7_spmd} | conditional | flops 4846722048 | bytes 49223464 | solution.py:294
  67.7 1.4 %reshape.160 = f32[2,4,4,32]{3,2,1,0:T(4,128)} reshape(f32[8,128]{1,0:T(8,128)} %param) | data formatting | bytes 8192 | tf_op jit(solution)/shard_map/reshape | solution.py:295
  69.1 0.7 copy.57
  69.8 0.6 slice_reduce_fusion.3
  70.4 0.1 stack_reshape_squeeze.56
  70.5 0.1 stack_reshape_squeeze.57
  70.6 0.1 stack_reshape_squeeze.58
  70.7 0.1 stack_reshape_squeeze.59
  70.8 1.3 %stack.47 = f32[8,2,2,2,128]{4,3,2,1,0:T(2,128)} pad(f32[8,2,2,1,128]{4,3,2,1,0:T(1,128)S(1)} %stack_broadcast_in_dim.2, f32[]{:T(128)} %slice_reduce_fusion.3), padding=0_0x0_0x0_0x0_1x0_0 | pad | bytes 49156 | tf_op jit(solution)/shard_map/stack | solution.py:304
  72.1 5.9 %all-to-all-start = ((f32[32,2,128]{2,1,0:T(2,128)}), f32[32,2,128]{2,1,0:T(2,128)S(1)}, u32[]{:S(2)}, u32[]{:S(2)}) async-start(f32[32,2,128]{2,1,0:T(2,128)} %bitcast.28), calls=%async_computation | async-start | bytes 65536 | tf_op jit(solution)/shard_map/all_to_all | solution.py:305
  78.1 7.2 %all-to-all-done = f32[32,2,128]{2,1,0:T(2,128)S(1)} async-done(((f32[32,2,128]{2,1,0:T(2,128)}), f32[32,2,128]{2,1,0:T(2,128)S(1)}, u32[]{:S(2)}, u32[]{:S(2)}) %all-to-all-start) | async-done | bytes 32800 | tf_op jit(solution)/shard_map/all_to_all | solution.py:305
  85.3 0.1 slice_reduce_fusion.1
  85.4 0.1 reshape.157
  85.5 0.6 copy.18
  86.1 0.1 copy.19
  86.2 0.6 reshape.159
  (56 shorter events, 0.5 us)
Async XLA Ops:
  0.6 3.5 %copy-start = (s32[4096]{0:T(1024)S(1)}, s32[4096]{0:T(1024)}, u32[]{:S(2)}) copy-start(s32[4096]{0:T(1024)} %param.16) | copy-start | bytes 49156
  0.7 2.3 %copy-start.5 = (s32[4096,32]{0,1:T(8,128)S(1)}, s32[4096,32]{0,1:T(8,128)}, u32[]{:S(2)}) copy-start(s32[4096,32]{0,1:T(8,128)} %param.15) | copy-start | bytes 1572868
  2.4 11.9 %copy-start.3 = (bf16[2048,256]{1,0:T(8,128)(2,1)}, bf16[2048,256]{1,0:T(8,128)(2,1)S(1)}, u32[]{:S(2)}) copy-start(bf16[2048,256]{1,0:T(8,128)(2,1)S(1)} %get-tuple-element.247.t0_ref) | copy-start | bytes 3145732
  2.4 1.2 %copy-start.11 = (bf16[256,256]{1,0:T(8,128)(2,1)S(1)}, bf16[256,256]{1,0:T(8,128)(2,1)}, u32[]{:S(2)}) copy-start(bf16[256,256]{1,0:T(8,128)(2,1)} %o0_ref.3) | copy-start | bytes 393220
  2.4 1.7 %copy-start.10 = (s32[4096]{0:T(1024)S(1)}, s32[4096]{0:T(1024)}, u32[]{:S(2)}) copy-start(s32[4096]{0:T(1024)} %param.17) | copy-start | bytes 49156
  2.5 3.5 %collective-permute-start.13 = (bf16[2048,256]{1,0:T(8,128)(2,1)S(1)}, bf16[2048,256]{1,0:T(8,128)(2,1)}, u32[]{:S(2)}, u32[]{:S(2)}) collective-permute-start(bf16[2048,256]{1,0:T(8,128)(2,1)S(1)} %get-tuple-element.246), channel_id=1, source_target_pairs={{0,1},{1,0},{2,3},{3,2},{4,5},{5,4},{6,7},{7,6},{8,9},{9,8},{10,11... | collective-permute-start | bytes 3145736 | tf_op jit(solution)/shard_map/ppermute | solution.py:165
  3.5 2.3 %collective-permute-start.15 = (bf16[32,2048]{1,0:T(8,128)(2,1)S(1)}, bf16[32,2048]{1,0:T(8,128)(2,1)S(1)}, u32[]{:S(2)}, u32[]{:S(2)}) collective-permute-start(bf16[32,2048]{1,0:T(8,128)(2,1)S(1)} %get-tuple-element.259), channel_id=1, source_target_pairs={{0,1},{1,0},{2,3},{3,2},{4,5},{5,4},{6,7},{7,6},{8,9},{9,8},{10,11... | collective-permute-start | bytes 393224 | tf_op jit(solution)/shard_map/ppermute | solution.py:165
  3.7 2.3 %collective-permute-start.14 = (bf16[256,256]{1,0:T(8,128)(2,1)S(1)}, bf16[256,256]{1,0:T(8,128)(2,1)S(1)}, u32[]{:S(2)}, u32[]{:S(2)}) collective-permute-start(bf16[256,256]{1,0:T(8,128)(2,1)S(1)} %copy-done.11), channel_id=1, source_target_pairs={{0,1},{1,0},{2,3},{3,2},{4,5},{5,4},{6,7},{7,6},{8,9},{9,8},{10,11... | collective-permute-start | bytes 393224 | tf_op jit(solution)/shard_map/ppermute | solution.py:165
  5.1 9.1 %copy-start.15 = (s32[16,128]{1,0:T(8,128)}, s32[16,128]{1,0:T(8,128)S(1)}, u32[]{:S(2)}) copy-start(s32[16,128]{1,0:T(8,128)S(1)} %get-tuple-element.188.pos_ref) | copy-start | bytes 24580
  5.9 8.3 %copy-start.6 = (bf16[80,2048]{1,0:T(8,128)(2,1)}, bf16[80,2048]{1,0:T(8,128)(2,1)S(1)}, u32[]{:S(2)}) copy-start(bf16[80,2048]{1,0:T(8,128)(2,1)S(1)} %maximum_maximum_fusion.codes_ref) | copy-start | bytes 983044
  6.0 8.3 %copy-start.13 = (bf16[256,256]{1,0:T(8,128)(2,1)}, bf16[256,256]{1,0:T(8,128)(2,1)S(1)}, u32[]{:S(2)}) copy-start(bf16[256,256]{1,0:T(8,128)(2,1)S(1)} %collective-permute-done.14.o1_ref) | copy-start | bytes 393220
  11.6 8.1 %collective-permute-start.16 = (bf16[64,1024]{1,0:T(8,128)(2,1)S(1)}, bf16[64,1024]{1,0:T(8,128)(2,1)S(1)}, u32[]{:S(2)}, u32[]{:S(2)}) collective-permute-start(bf16[64,1024]{1,0:T(8,128)(2,1)S(1)} %slice.176), channel_id=1, source_target_pairs={{0,2},{1,3},{2,0},{3,1},{4,6},{5,7},{6,4},{7,5},{8,10},{9,11},{10,... | collective-permute-start | bytes 393224 | tf_op jit(solution)/shard_map/ppermute | solution.py:165
  19.8 17.7 %copy-start.8 = (f32[256]{0:T(256)S(1)}, f32[256]{0:T(256)}, u32[]{:S(2)}) copy-start(f32[256]{0:T(256)} %param.14) | copy-start | bytes 3076
  19.8 4.8 %collective-permute-start.17 = (bf16[144,256]{1,0:T(8,128)(2,1)S(1)}, bf16[144,256]{1,0:T(8,128)(2,1)S(1)}, u32[]{:S(2)}, u32[]{:S(2)}) collective-permute-start(bf16[144,256]{1,0:T(8,128)(2,1)S(1)} %get-tuple-element.253), channel_id=1, source_target_pairs={{0,8},{4,12},{8,0},{12,4},{16,24},{20,28},{24,16},{28,20},{1,9},{5... | collective-permute-start | bytes 221192 | tf_op jit(solution)/shard_map/ppermute | solution.py:165
  21.4 8.9 %collective-permute-start.18 = (bf16[144,256]{1,0:T(8,128)(2,1)S(1)}, bf16[144,256]{1,0:T(8,128)(2,1)S(1)}, u32[]{:S(2)}, u32[]{:S(2)}) collective-permute-start(bf16[144,256]{1,0:T(8,128)(2,1)S(1)} %get-tuple-element.252), channel_id=1, source_target_pairs={{0,16},{4,20},{8,24},{12,28},{16,0},{20,4},{24,8},{28,12},{1,17},{... | collective-permute-start | bytes 221192 | tf_op jit(solution)/shard_map/ppermute | solution.py:165
  24.0 6.3 %collective-permute-start.19 = (bf16[144,256]{1,0:T(8,128)(2,1)S(1)}, bf16[144,256]{1,0:T(8,128)(2,1)S(1)}, u32[]{:S(2)}, u32[]{:S(2)}) collective-permute-start(bf16[144,256]{1,0:T(8,128)(2,1)S(1)} %get-tuple-element.251), channel_id=1, source_target_pairs={{0,24},{4,28},{8,16},{12,20},{16,8},{20,12},{24,0},{28,4},{1,25},{... | collective-permute-start | bytes 221192 | tf_op jit(solution)/shard_map/ppermute | solution.py:165
  24.2 13.2 %collective-permute-start.22 = (s16[1024,256]{1,0:T(8,128)(2,1)S(1)}, s16[1024,256]{1,0:T(8,128)(2,1)S(1)}, u32[]{:S(2)}, u32[]{:S(2)}) collective-permute-start(s16[1024,256]{1,0:T(8,128)(2,1)S(1)} %get-tuple-element.192), channel_id=1, source_target_pairs={{0,2},{1,3},{2,0},{3,1},{4,6},{5,7},{6,4},{7,5},{8,10},{9,11},{10,... | collective-permute-start | bytes 1572872 | tf_op jit(solution)/shard_map/ppermute | solution.py:165
  30.4 5.4 %collective-permute-start.20 = (bf16[80,1024]{1,0:T(8,128)(2,1)S(1)}, bf16[80,1024]{1,0:T(8,128)(2,1)S(1)}, u32[]{:S(2)}, u32[]{:S(2)}) collective-permute-start(bf16[80,1024]{1,0:T(8,128)(2,1)S(1)} %pad_maximum_fusion.14), channel_id=1, source_target_pairs={{0,4},{4,0},{8,12},{12,8},{16,20},{20,16},{24,28},{28,24},{1,5},{5... | collective-permute-start | bytes 491528 | tf_op jit(solution)/shard_map/ppermute | solution.py:165
  38.4 6.1 %collective-permute-start.23 = (bf16[256,256]{1,0:T(8,128)(2,1)S(1)}, bf16[256,256]{1,0:T(8,128)(2,1)S(1)}, u32[]{:S(2)}, u32[]{:S(2)}) collective-permute-start(bf16[256,256]{1,0:T(8,128)(2,1)S(1)} %get-tuple-element.194), channel_id=1, source_target_pairs={{0,8},{4,12},{8,0},{12,4},{16,24},{20,28},{24,16},{28,20},{1,9},{5... | collective-permute-start | bytes 393224 | tf_op jit(solution)/shard_map/ppermute | solution.py:165
  39.1 12.4 %collective-permute-start.24 = (bf16[256,256]{1,0:T(8,128)(2,1)S(1)}, bf16[256,256]{1,0:T(8,128)(2,1)S(1)}, u32[]{:S(2)}, u32[]{:S(2)}) collective-permute-start(bf16[256,256]{1,0:T(8,128)(2,1)S(1)} %get-tuple-element.195), channel_id=1, source_target_pairs={{0,16},{4,20},{8,24},{12,28},{16,0},{20,4},{24,8},{28,12},{1,17},{... | collective-permute-start | bytes 393224 | tf_op jit(solution)/shard_map/ppermute | solution.py:165
  42.6 8.8 %collective-permute-start.25 = (bf16[256,256]{1,0:T(8,128)(2,1)S(1)}, bf16[256,256]{1,0:T(8,128)(2,1)S(1)}, u32[]{:S(2)}, u32[]{:S(2)}) collective-permute-start(bf16[256,256]{1,0:T(8,128)(2,1)S(1)} %get-tuple-element.196), channel_id=1, source_target_pairs={{0,24},{4,28},{8,16},{12,20},{16,8},{20,12},{24,0},{28,4},{1,25},{... | collective-permute-start | bytes 393224 | tf_op jit(solution)/shard_map/ppermute | solution.py:165
  51.5 10.2 %collective-permute-start.26 = (bf16[1024,256]{1,0:T(8,128)(2,1)S(1)}, bf16[1024,256]{1,0:T(8,128)(2,1)S(1)}, u32[]{:S(2)}, u32[]{:S(2)}) collective-permute-start(bf16[1024,256]{1,0:T(8,128)(2,1)S(1)} %constant_dynamic-update-slice_fusion.8.refs_0_), channel_id=1, source_target_pairs={{0,4},{4,0},{8,12},{12,8},{16,20},{20,16},{24,28},{28,24},{1,5},{5... | collective-permute-start | bytes 1572872 | tf_op jit(solution)/shard_map/ppermute | solution.py:165
  53.1 8.6 %collective-permute-start.21 = (bf16[48,2048]{1,0:T(8,128)(2,1)S(1)}, bf16[48,2048]{1,0:T(8,128)(2,1)S(1)}, u32[]{:S(2)}, u32[]{:S(2)}) collective-permute-start(bf16[48,2048]{1,0:T(8,128)(2,1)S(1)} %pad_maximum_fusion.13), channel_id=1, source_target_pairs={{0,1},{1,0},{2,3},{3,2},{4,5},{5,4},{6,7},{7,6},{8,9},{9,8},{10,11... | collective-permute-start | bytes 589832 | tf_op jit(solution)/shard_map/ppermute | solution.py:165
  53.2 9.8 %collective-permute-start.27 = (bf16[1024,256]{1,0:T(8,128)(2,1)S(1)}, bf16[1024,256]{1,0:T(8,128)(2,1)S(1)}, u32[]{:S(2)}, u32[]{:S(2)}) collective-permute-start(bf16[1024,256]{1,0:T(8,128)(2,1)S(1)} %constant_dynamic-update-slice_fusion.8.refs_0_), channel_id=1, source_target_pairs={{0,1},{1,0},{2,3},{3,2},{4,5},{5,4},{6,7},{7,6},{8,9},{9,8},{10,11... | collective-permute-start | bytes 1572872 | tf_op jit(solution)/shard_map/ppermute | solution.py:165
  61.6 1.9 %collective-permute-start.28 = (bf16[1024,256]{1,0:T(8,128)(2,1)S(1)}, bf16[1024,256]{1,0:T(8,128)(2,1)S(1)}, u32[]{:S(2)}, u32[]{:S(2)}) collective-permute-start(bf16[1024,256]{1,0:T(8,128)(2,1)S(1)} %collective-permute-done.26.refs_1_), channel_id=1, source_target_pairs={{0,1},{1,0},{2,3},{3,2},{4,5},{5,4},{6,7},{7,6},{8,9},{9,8},{10,11... | collective-permute-start | bytes 1572872 | tf_op jit(solution)/shard_map/ppermute | solution.py:165
  72.1 13.2 %all-to-all-start = ((f32[32,2,128]{2,1,0:T(2,128)}), f32[32,2,128]{2,1,0:T(2,128)S(1)}, u32[]{:S(2)}, u32[]{:S(2)}) async-start(f32[32,2,128]{2,1,0:T(2,128)} %bitcast.28), calls=%async_computation | async-start | bytes 65536 | tf_op jit(solution)/shard_map/all_to_all | solution.py:305

commit v2 on v0

v2 whole, which is shorter than its diff:
```python
import functools
import math

import jax
import jax.numpy as jnp
from jax import lax
from jax.experimental import pallas as pl
from jax.experimental.pallas import tpu as pltpu
from jax.sharding import PartitionSpec as P

BINS = 32
NODES = 8
LANES = 128
EXTRA = 16
STEPS = 65536.0
PARAMS = pltpu.CompilerParams(vmem_limit_bytes=32 * 1024 * 1024)
VMEM = pl.BlockSpec(memory_space=pltpu.VMEM)
SMEM = pl.BlockSpec(memory_space=pltpu.SMEM)


def rank_of(node, live):
    groups = node.shape[0]
    block = groups * LANES
    members = [jnp.where((node == n) & live, 1.0, 0.0) for n in range(NODES)]
    member = jnp.concatenate(members, axis=0)
    size = NODES * groups
    i = lax.broadcasted_iota(jnp.int32, (LANES, LANES), 0)
    j = lax.broadcasted_iota(jnp.int32, (LANES, LANES), 1)
    before = jnp.where(i < j, 1.0, 0.0).astype(jnp.bfloat16)
    inside = jnp.dot(member.astype(jnp.bfloat16), before, preferred_element_type=jnp.float32)
    count = jnp.sum(member, axis=1, keepdims=True)
    p = lax.broadcasted_iota(jnp.int32, (size, size), 0)
    q = lax.broadcasted_iota(jnp.int32, (size, size), 1)
    earlier = jnp.where((p // groups == q // groups) & (q < p), 1.0, 0.0).astype(jnp.bfloat16)
    spread = jnp.broadcast_to(count, (size, LANES))
    base = jnp.dot(earlier, spread.astype(jnp.bfloat16), preferred_element_type=jnp.float32)
    rank = inside + base
    pos = jnp.zeros((groups, LANES), jnp.float32)
    for n in range(NODES):
        pos += members[n] * (rank[n * groups : (n + 1) * groups] + float(n * block))
    return jnp.where(live, pos, -1.0).astype(jnp.int32), jnp.max(base + spread).astype(jnp.int32)


def choose_rows(pos_ref, pick, distance, slots, room, x, a, turn):
    groups = pos_ref.shape[0]
    block = groups * LANES
    for slot in range(slots):
        node = (x ^ distance) * slots + (a ^ slot)
        start = node * block + turn * room
        wanted = start + lax.broadcasted_iota(jnp.int32, (room, LANES), 0)
        for g in range(groups):
            pick[slot * room : (slot + 1) * room, g * LANES : (g + 1) * LANES] = jnp.where(
                pos_ref[g : g + 1, :] == wanted, 1.0, 0.0
            ).astype(jnp.bfloat16)


def moved(codes, pick):
    return lax.dot_general(codes, pick, (((1,), (1,)), ((), ())), preferred_element_type=jnp.float32)


def theirs_kernel(targets_ref, theirs_ref, sem):
    block = theirs_ref.shape[0]
    first = pl.multiple_of((1 - (lax.axis_index("feat") & 1)) * block, block)
    copy = pltpu.make_async_copy(targets_ref.at[pl.ds(first, block), :], theirs_ref, sem)
    copy.start()
    copy.wait()


def prepare_kernel(copies, codes_ref, boot_ref, give_ref, mine_ref):
    block = mine_ref.shape[1]
    features = codes_ref.shape[0]
    part = features // copies
    core = lax.axis_index("feat") & 1
    minor = lax.axis_index("rows") & (copies - 1)
    mine, theirs = pl.multiple_of(core * block, block), pl.multiple_of((1 - core) * block, block)
    for out_ref, first in ((give_ref, theirs), (mine_ref, mine)):
        parts = [codes_ref[pl.ds((minor ^ d) * part, part), pl.ds(first, block)] for d in range(copies)]
        out_ref[:features, :] = jnp.concatenate(parts, axis=0).astype(jnp.float32).astype(jnp.bfloat16)
    mine_ref[features:, :] = jnp.zeros((EXTRA, block), jnp.bfloat16)
    first = pl.multiple_of(core * (block // LANES), block // LANES)
    weights = boot_ref[pl.ds(first, block // LANES), :].astype(jnp.float32)
    line = lax.broadcasted_iota(jnp.int32, (EXTRA, LANES), 0)
    for g in range(block // LANES):
        row = jnp.where(line == 0, weights[g : g + 1, :], 0.0)
        mine_ref[features:, g * LANES : (g + 1) * LANES] = row.astype(jnp.bfloat16)


def order_kernel(chips, slots, room, turn_ref, node_ref, boot_ref, mine_ref, taken_ref, pos_ref, rounds_ref, *outs):
    feat, place = lax.axis_index("feat"), lax.axis_index("rows")
    groups = pos_ref.shape[0]
    first = pl.multiple_of((feat & 1) * groups, groups)
    pos, most = rank_of(node_ref[pl.ds(first, groups), :], boot_ref[pl.ds(first, groups), :] > 0)
    pos_ref[...] = pos
    rounds_ref[0] = (most + (room - 1)) // room
    features = taken_ref.shape[0]
    codes = jnp.concatenate([mine_ref[:features, :], taken_ref[...]], axis=0)
    for distance in range(1, chips):
        pick, sorted_ref = outs[2 * distance - 2 : 2 * distance]
        choose_rows(pos_ref, pick, distance, slots, room, feat >> 1, major_of(place, slots), turn_ref[0])
        sorted_ref[...] = moved(codes, pick[...]).astype(jnp.bfloat16)


def major_of(place, slots):
    copies = lax.axis_size("rows") // slots
    return place >> (copies.bit_length() - 1)


def turns_of(pick, targets_ref, t0, t1_ref, o0_ref, o1_ref, sem):
    block = t0.shape[0]
    first = pl.multiple_of((lax.axis_index("feat") & 1) * block, block)
    copy = pltpu.make_async_copy(targets_ref.at[pl.ds(first, block), :], t0, sem)
    copy.start()
    s1 = jnp.dot(pick[...], t1_ref[...], preferred_element_type=jnp.float32).astype(jnp.bfloat16)
    partial = jnp.dot(s1, o1_ref[...], preferred_element_type=jnp.float32)
    copy.wait()
    s0 = jnp.dot(pick[...], t0[...], preferred_element_type=jnp.float32).astype(jnp.bfloat16)
    partial += jnp.dot(s0, o0_ref[...], preferred_element_type=jnp.float32)
    turns = partial * (0.5 / math.pi)
    return turns - jnp.floor(turns)


def send_kernel(rounds_ref, pick_ref, targets_ref, t1_ref, o0_ref, o1_ref, *refs):
    outs, (passed_ref, t0, sem) = refs[:-3], refs[-3:]
    passed_ref[0] = rounds_ref[0]
    turns = turns_of(pick_ref, targets_ref, t0, t1_ref, o0_ref, o1_ref, sem)
    coded = (jnp.minimum((turns * STEPS).astype(jnp.int32), 65535) - 32768).astype(jnp.int16)
    first = 0
    for out_ref in outs:
        out_ref[...] = coded[first : first + out_ref.shape[0]]
        first += out_ref.shape[0]


def codes_kernel(chips, slots, room, turn_ref, rounds_ref, pos_ref, mine_ref, taken_ref, *refs):
    received, pick, pieces = refs[: chips - 1], refs[chips - 1], refs[chips:]
    feat, place = lax.axis_index("feat"), lax.axis_index("rows")
    choose_rows(pos_ref, pick, 0, slots, room, feat >> 1, major_of(place, slots), turn_ref[0])
    features = taken_ref.shape[0]
    both = 2 * features
    codes = jnp.concatenate([mine_ref[:features, :], taken_ref[...], mine_ref[features:, :]], axis=0)
    own = moved(codes, pick[...])
    line = lax.broadcasted_iota(jnp.int32, own.shape, 0)
    own = jnp.where(line == both + 1, rounds_ref[0].astype(jnp.float32), own).astype(jnp.bfloat16)
    for slot in range(slots):
        span = slice(slot * room, (slot + 1) * room)
        pieces[slot][: both + EXTRA, :] = own[:, span]
        for d in range(1, chips):
            first = both * d + EXTRA
            pieces[slot][first : first + both, :] = received[d - 1][:, span]


def keep_kernel(pick_ref, targets_ref, t1_ref, o0_ref, o1_ref, out_ref, t0, sem):
    out_ref[...] = turns_of(pick_ref, targets_ref, t0, t1_ref, o0_ref, o1_ref, sem)


def cosine_kernel(chips, first, own_ref, phase_ref, *refs):
    received, outs = refs[: chips - 1], refs[chips - 1 :]
    width = phase_ref.shape[1]
    room = outs[0].shape[0]
    scaling = math.sqrt(2.0 / width)
    series = [(-1.0) ** (k + 1) * (2 * math.pi) ** (2 * k + 1) / math.factorial(2 * k + 1) for k in range(7)]
    shift = phase_ref[...] * (0.5 / math.pi)
    for slot, out_ref in enumerate(outs):
        turns = own_ref[(first + slot) * room : (first + slot + 1) * room, :] + shift
        for ref in received:
            turns += (ref[slot * room : (slot + 1) * room, :].astype(jnp.float32) + 32768.5) * (1.0 / STEPS)
        turns = jnp.abs(turns - jnp.floor(turns + 0.5)) - 0.25
        square = turns * turns
        value = jnp.full_like(turns, series[-1])
        for term in series[-2::-1]:
            value = value * square + term
        out_ref[...] = (scaling * (value * turns)).astype(jnp.bfloat16)


def far_cosine_kernel(chips, first, slots, own_ref, phase_ref, *refs):
    split = chips - 1 + slots
    pieces, codes_ref = refs[chips - 1 : split], refs[-1]
    cosine_kernel(chips, first, own_ref, phase_ref, *refs[: chips - 1], *refs[split:-1])
    room = pieces[0].shape[1]
    for slot, piece in enumerate(pieces):
        codes_ref[:, slot * room : (slot + 1) * room] = piece[...]


def gains_of(left, counts):
    whole = left[..., BINS - 1 :, :]
    total = counts[..., BINS - 1 :, :]
    other = total - counts
    differ = left * (1.0 / jnp.maximum(counts, 1.0)) - (whole - left) * (1.0 / jnp.maximum(other, 1.0))
    return (counts * other / total) * jnp.sum(differ * differ, axis=-1, keepdims=True)


def add_rows(features, offset, weight_at, codes_ref, pieces, table, left_ref, counts_ref, fresh):
    room = pieces[0].shape[0]
    length = room * len(pieces)
    threshold = lax.broadcasted_iota(jnp.int32, (BINS, length), 0).astype(jnp.float32)
    codes = codes_ref[...].astype(jnp.float32)
    weight = codes[weight_at : weight_at + 1, :]
    for f in range(features):
        rows = slice(f * BINS, (f + 1) * BINS)
        entry = jnp.where(codes[offset + f : offset + f + 1, :] <= threshold, weight, 0.0)
        table[rows, :] = entry.astype(jnp.bfloat16)
        folded = entry[:, :LANES]
        for g in range(1, length // LANES):
            folded += entry[:, g * LANES : (g + 1) * LANES]
        counts_ref[rows, :] = folded if fresh else counts_ref[rows, :] + folded
    block = jnp.concatenate([piece[...] for piece in pieces], axis=0)
    sums = jnp.dot(table[...], block, preferred_element_type=jnp.float32)
    left_ref[...] = sums if fresh else left_ref[...] + sums


def sums_kernel(features, first, copies, *refs):
    sides, pieces, earlier = refs[: 2 * copies], refs[2 * copies : 4 * copies], refs[4 * copies : -3]
    left_ref, counts_ref, table = refs[-3:]
    add_rows(features, first, sides, pieces, earlier, left_ref, counts_ref, table)


def add_rows(features, first, sides, pieces, earlier, left_ref, counts_ref, table):
    rows = pieces[0].shape[0]
    span = slice(first, first + rows)
    length = rows * len(pieces)
    threshold = lax.broadcasted_iota(jnp.int32, (BINS, length), 0).astype(jnp.float32)
    codes, weights = [], []
    for index, side in enumerate(sides):
        lines = side[:, span].astype(jnp.float32)
        codes_at, weight_at = (EXTRA, 0) if index % 2 else (0, features)
        codes.append(lines[codes_at : codes_at + features])
        weights.append(lines[weight_at : weight_at + 1])
    codes, weight = jnp.concatenate(codes, axis=1), jnp.concatenate(weights, axis=1)
    for f in range(features):
        rows = slice(f * BINS, (f + 1) * BINS)
        entry = jnp.where(codes[f : f + 1, :] <= threshold, weight, 0.0)
        table[rows, :] = entry.astype(jnp.bfloat16)
        folded = entry[:, :LANES]
        for g in range(1, length // LANES):
            folded += entry[:, g * LANES : (g + 1) * LANES]
        counts_ref[rows, :] = earlier[1][rows, :] + folded if earlier else folded
    block = jnp.concatenate([piece[...] for piece in pieces], axis=0)
    sums = jnp.dot(table[...], block, preferred_element_type=jnp.float32)
    left_ref[...] = earlier[0][...] + sums if earlier else sums


def gains_kernel(features, first, copies, lines, sets, groups, chips, *refs):
    sides, pieces, earlier = refs[: 2 * copies], refs[2 * copies : 4 * copies], refs[4 * copies : -5]
    left_ref, counts_ref, send_ref, needed_ref, table = refs[-5:]
    add_rows(features, first, sides, pieces, earlier, left_ref, counts_ref, table)
    needed = 0.0
    for index, side in enumerate(sides):
        flags_at = 0 if index % 2 else features
        flags = side[flags_at : flags_at + EXTRA, :].astype(jnp.float32)
        line = lax.broadcasted_iota(jnp.int32, flags.shape, 0)
        needed = jnp.maximum(needed, jnp.max(jnp.where(line == 1, flags, 0.0)))
    needed_ref[0] = needed.astype(jnp.int32)
    x = lax.axis_index("feat") >> 1
    columns = []
    largest = jnp.zeros((1, 1), jnp.float32)
    threshold = lax.broadcasted_iota(jnp.int32, (BINS, 1), 0)
    for f in range(features):
        rows = slice(f * BINS, (f + 1) * BINS)
        counts = jnp.sum(counts_ref[rows, :], axis=1, keepdims=True)
        column = gains_of(left_ref[rows, :], counts)
        column = jnp.where(threshold < BINS - 1, column, 0.0)
        largest = jnp.maximum(largest, jnp.max(column, axis=0, keepdims=True))
        columns.append(column)
    load = send_ref.shape[2]
    wide = load // BINS
    fill = jnp.broadcast_to(largest, (BINS, 1))
    i = lax.broadcasted_iota(jnp.int32, (load, load), 0)
    j = lax.broadcasted_iota(jnp.int32, (load, load), 1)
    for d in range(chips):
        for line in range(lines):
            first = (d * lines + line) * wide
            column = jnp.concatenate([jnp.where(threshold < BINS - 1, c, fill) for c in columns[first : first + wide]], axis=0)
            row = jnp.sum(jnp.where(i == j, column, 0.0), axis=0, keepdims=True)
            for place in range(groups):
                if place // (groups // sets) % lines == line:
                    for core in range(2):
                        send_ref[place * 2 * chips + 2 * (x ^ d) + core] = row


def finish_kernel(chips, slots, copies, lines, sets, groups, got_ref, gains_ref, best_ref, rows_ref):
    feat, place = lax.axis_index("feat"), lax.axis_index("rows")
    core = feat & 1
    per_set = groups // sets
    source = (place >> (per_set.bit_length() - 1)) >> (lines.bit_length() - 1)
    load = got_ref.shape[2]
    own, top = [], []
    for node in range(NODES):
        x, a = node // slots, node % slots
        index = lambda b, c: (a * copies + b) * 2 * chips + 2 * x + c
        own.append(got_ref[index(source, core)])
        largest = got_ref[index(0, 0)]
        for b in range(copies):
            for c in range(2):
                largest = jnp.maximum(largest, got_ref[index(b, c)])
        top.append(largest)
    own, top = jnp.concatenate(own, axis=0), jnp.concatenate(top, axis=0)
    for f in range(load // BINS):
        rows_ref[f * NODES : (f + 1) * NODES, :] = own[:, f * BINS : (f + 1) * BINS - 1]
    owned = gains_ref.shape[0]
    first = (place * owned) & (rows_ref.shape[0] - 1)
    gains_ref[...] = rows_ref[pl.ds(first, owned), :]
    i = lax.broadcasted_iota(jnp.int32, (NODES, NODES), 0)
    j = lax.broadcasted_iota(jnp.int32, (NODES, NODES), 1)
    best_ref[...] = jnp.sum(jnp.where(i == j, top[:, BINS - 1 : BINS], 0.0), axis=0, keepdims=True)


def split_rows(mesh_sizes, targets, omega, phase, codes, node, boot_counts):
    groups_all, feat_all = mesh_sizes
    chips = feat_all // 2
    slots = NODES // chips
    copies = groups_all // slots
    rows_dev, feat_dev = codes.shape
    width = omega.shape[1]
    block = rows_dev // 2
    room = block // NODES
    owned = feat_dev * NODES // groups_all
    per_owner = max(1, owned // NODES)
    sets = feat_dev // per_owner
    lines = sets // copies
    part = lines * per_owner
    features = chips * part

    feat = lax.axis_index("feat")
    x = feat // 2
    both = 2 * feat_dev
    span = slots * room
    load = per_owner * BINS
    columns = targets.shape[1]

    def permute(axis, size, distance, array):
        return lax.ppermute(array, axis, [(i, i ^ distance) for i in range(size)])

    swap = functools.partial(permute, "feat", feat_all, 1)

    def along_x(distance, array):
        return permute("feat", feat_all, 2 * distance, array)

    def along_major(distance, array):
        return permute("rows", groups_all, copies * distance, array)

    def along_minor(distance, array):
        return permute("rows", groups_all, distance, array)

    def shaped(kind, *shape):
        return jax.ShapeDtypeStruct(shape, kind)

    def kernel(body, name, outs, scratch=(), micros=0.0, **more):
        def call(*arrays):
            ins = [SMEM if a.shape == (1,) else pl.BlockSpec(memory_space=pl.ANY) if a is targets else VMEM for a in arrays]
            return pl.pallas_call(
                body, out_shape=tuple(outs), in_specs=ins, scratch_shapes=list(scratch), compiler_params=PARAMS, name=name,
                out_specs=tuple(SMEM if out.shape == (1,) else VMEM for out in outs),
                cost_estimate=pl.CostEstimate(flops=int(micros * 1e9), bytes_accessed=1 << 16, transcendentals=0), **more,
            )(*arrays)

        return call

    half_targets = [pltpu.VMEM((block, columns), jnp.bfloat16), pltpu.SemaphoreType.DMA(())]
    first_round = jnp.zeros((1,), jnp.int32)
    node_lines = node.reshape(rows_dev // LANES, LANES)
    boot_lines = boot_counts.reshape(rows_dev // LANES, LANES)
    (theirs,) = kernel(
        theirs_kernel, "theirs", [shaped(jnp.bfloat16, block, columns)], [pltpu.SemaphoreType.DMA(())]
    )(targets)
    theirs = swap(theirs)
    give, mine = kernel(
        functools.partial(prepare_kernel, copies), "prepare",
        [shaped(jnp.bfloat16, feat_dev, block), shaped(jnp.bfloat16, feat_dev + EXTRA, block)], micros=1.0,
    )(codes.T, boot_lines)
    taken, omega_theirs = swap(give), swap(omega)
    near = slots // 2
    parts = [near, slots - near]

    def one_round(turn):
        outs = [shaped(jnp.int32, block // LANES, LANES), shaped(jnp.int32, 1)]
        for d in range(1, chips):
            outs += [shaped(jnp.bfloat16, span, block), shaped(jnp.bfloat16, both, span)]
        pos, rounds, *chosen = kernel(functools.partial(order_kernel, chips, slots, room), "order", outs, micros=3.0)(
            turn, node_lines, boot_lines, mine, taken
        )
        chip_codes = [along_x(d, chosen[2 * d - 1]) for d in range(1, chips)]
        angles = []
        for d in range(1, chips):
            outs = [shaped(jnp.int16, n * room, width) for n in parts] + [shaped(jnp.int32, 1)]
            *sent, rounds = kernel(send_kernel, "send", outs, half_targets, 4.0)(
                rounds, chosen[2 * d - 2], targets, theirs, omega, omega_theirs
            )
            angles.append([along_x(d, s) for s in sent])
        pick, *pieces = kernel(
            functools.partial(codes_kernel, chips, slots, room), "codes",
            [shaped(jnp.bfloat16, span, block)] + [shaped(jnp.bfloat16, chips * both + EXTRA, room)] * slots, micros=3.0,
        )(turn, rounds, pos, mine, taken, *chip_codes)
        pieces = [along_major(d, pieces[d]) if d else pieces[d] for d in range(slots)]
        (own_angles,) = kernel(keep_kernel, "keep", [shaped(jnp.float32, span, width)], half_targets, 4.0)(
            pick, targets, theirs, omega, omega_theirs
        )
        line = phase.reshape(1, width)
        *far, node_codes = kernel(
            functools.partial(far_cosine_kernel, chips, near, slots), "cosine",
            [shaped(jnp.bfloat16, room, width)] * parts[1] + [shaped(jnp.bfloat16, chips * both + EXTRA, span)], micros=1.0,
        )(own_angles, line, *[a[1] for a in angles], *pieces)
        far = [along_major(near + i, f) for i, f in enumerate(far)]
        close = kernel(
            functools.partial(cosine_kernel, chips, 0), "cosine", [shaped(jnp.bfloat16, room, width)] * near, micros=1.0
        )(own_angles, line, *[a[0] for a in angles])
        close = [along_major(d, f) if d else f for d, f in enumerate(close)]

        extras = node_codes[both : both + EXTRA]
        by_part = jnp.concatenate([node_codes[:both], node_codes[both + EXTRA :]], axis=0)
        by_part = by_part.reshape(chips, 2, copies, part, span)
        sides = []
        for d in range(copies):
            nearer = by_part[:, 0, d].reshape(features, span)
            farther = by_part[:, 1, d].reshape(features, span)
            held = jnp.concatenate([nearer, extras, farther], axis=0)
            held = along_minor(d, held) if d else held
            sides += [held[: features + EXTRA], swap(held[features:])]
        sums = [shaped(jnp.float32, features * BINS, width), shaped(jnp.float32, features * BINS, LANES)]
        state = ()
        for part_of, first in ((close, 0), (far, near * room)):
            mine_here = jnp.concatenate(part_of, axis=0)
            rows = []
            for d in range(copies):
                here = along_minor(d, mine_here) if d else mine_here
                rows += [here, swap(here)]
            last = part_of is far
            if last:
                body = functools.partial(gains_kernel, features, first, copies, lines, sets, groups_all, chips)
                outs = sums + [shaped(jnp.float32, groups_all * feat_all, 1, load), shaped(jnp.int32, 1)]
            else:
                body, outs = functools.partial(sums_kernel, features, first, copies), sums
            at = len(sides) + len(rows)
            scratch = [pltpu.VMEM((features * BINS, 2 * copies * mine_here.shape[0]), jnp.bfloat16)]
            state = kernel(
                body, "gains" if last else "sums", outs, scratch, 4.0,
                input_output_aliases={at: 0, at + 1: 1} if state else {},
            )(*sides, *rows, *state)
        return state

    left, counts, send, needed = one_round(first_round)

    def more_rounds():
        def step(state):
            turn, left, counts = state
            more_left, more_counts, _, _ = one_round(turn)
            return turn + 1, left + more_left, counts + more_counts

        _, all_left, all_counts = lax.while_loop(lambda state: state[0][0] < needed[0], step, (first_round + 1, left, counts))
        tallies = jnp.sum(all_counts, axis=1).reshape(features, BINS, 1)
        gains = gains_of(all_left.reshape(features, BINS, width), tallies).reshape(chips, lines, per_owner, BINS)
        last = jnp.arange(BINS) == BINS - 1
        gains = jnp.where(last, jnp.max(jnp.where(last, 0.0, gains)), gains)
        gains = jnp.stack([lax.dynamic_index_in_dim(gains, x ^ d, 0, keepdims=False) for d in range(chips)])
        line_of = [place // (groups_all // sets) % lines for place in range(groups_all)]
        rows = jnp.stack([gains[:, line].reshape(chips, 1, load) for line in line_of])
        return jnp.broadcast_to(rows, (groups_all, chips, 2, load)).reshape(send.shape)

    send = lax.cond(needed[0] > 1, more_rounds, lambda: send)
    got = lax.all_to_all(send, ("rows", "feat"), 0, 0)
    gains, best = kernel(
        functools.partial(finish_kernel, chips, slots, copies, lines, sets, groups_all), "finish",
        [shaped(jnp.float32, owned, BINS - 1), shaped(jnp.float32, 1, NODES)],
        [pltpu.VMEM((per_owner * NODES, BINS - 1), jnp.float32)],
    )(got)
    return gains, best.reshape(NODES)


def solution(mesh):
    in_specs = (P("rows", "feat"), P("feat", None), P(), P("rows", "feat"), P("rows"), P("rows"))
    out_specs = (P(("feat", "rows"), None), P())
    sizes = (mesh.shape["rows"], mesh.shape["feat"])
    return jax.shard_map(
        functools.partial(split_rows, sizes), mesh=mesh, in_specs=in_specs, out_specs=out_specs, check_vma=False
    )
```

time: 493 us -> 72.7 us (0.15)
  waiting for transfers between devices: 283 us -> 14.7 us
  blocking collectives: 90.3 us -> 12.4 us
  matrix products: 64.5 us -> 0 us
  other arithmetic: 27.3 us -> 0.04 us
  Pallas kernels: 0 us -> 22.6 us
  starting transfers between devices: 0.08 us -> 19.4 us
  between operations: 14.1 us -> 1.7 us
  local copies, waits for them, and re-layouts: 13.5 us -> 1.22 us
    psum x1 -> x0, waiting for transfers between devices: 230 us -> none  [body(): summed, summed_tallies = lax.psum((histogram, tallies), 'rows')]
    dot_general x33 -> x0, matrix products: 64.5 us -> none  [the longest x32 46.6 us: one_feature(): lax.dot_general(table, fourier, (((1,), (1,)), ((), ())), preferred_eleme...]
    all_gather x1 -> x0, waiting for transfers between devices: 52.3 us -> none  [body(): whole_targets = lax.all_gather(targets, 'feat', axis=1, tiled=True)]
    psum x1 -> x0, blocking collectives: 42.1 us -> none  [body(): summed, summed_tallies = lax.psum((histogram, tallies), 'rows')]
    pmax x1 -> x0, blocking collectives: 39.3 us -> none  [body(): best = lax.pmax(local_best, ('rows', 'feat'))]
    pallas_call x0 -> x11, Pallas kernels: none -> 22.6 us  [call(): pl.pallas_call(body, out_shape=tuple(outs), in_specs=ins, scratch_shapes=...]
    reduce_sum x35 -> x0, other arithmetic: 22.2 us -> none  [the longest x32 20.3 us: one_feature(): tallies = jnp.sum(table, axis=1, dtype=jnp.float32)]
    ppermute x0 -> x21, starting transfers between devices: none -> 19.4 us  [permute(): return lax.ppermute(array, axis, [(i, i ^ distance) for i in range(size)])]
  transfers between devices with their start and end apart: 2 -> 21, of which waited for: 2 -> 6; matrix products, arithmetic and copies ran while one was open for 1% -> 0% of each run, Pallas kernels for 0% -> 17%
where the time goes in v2:
time: 72.7 us; the launch traced here: 72.4 us
  Pallas kernels  22.6 us (31%)
  starting transfers between devices  19.4 us (27%)
  waiting for transfers between devices  14.7 us (20%)
  blocking collectives  12.4 us (17%)
  between operations  1.7 us (2%)
  local copies, waits for them, and re-layouts  1.22 us (2%)
    pallas_call x11, Pallas kernels, call(): pl.pallas_call(body, out_shape=tuple(outs), in_specs=ins, scratch_shapes=...  22.6 us
    ppermute x21, starting transfers between devices, permute(): return lax.ppermute(array, axis, [(i, i ^ distance) for i in range(size)])  19.4 us
    ppermute x21, waiting for transfers between devices, permute(): return lax.ppermute(array, axis, [(i, i ^ distance) for i in range(size)])  14.7 us
    all_to_all x1, blocking collectives, split_rows(): got = lax.all_to_all(send, ('rows', 'feat'), 0, 0)  12.4 us
  transfers between devices with their start and end apart: 21, of which 6 were waited for; matrix products, arithmetic and copies ran while one was open for 0% of the time, Pallas kernels for 17%

profile of v2, /device:TPU:0, one launch (start us, length us, event | category | flops | bytes accessed | tf_op | source)
XLA Modules:
  0.0 72.4 jit_solution(10638888987631415674)
XLA Ops:
  0.6 0.0 copy-start.13
  0.6 0.0 copy-start.5
  0.7 0.0 copy-start.11
  0.7 1.3 %theirs.1 = bf16[2048,256]{1,0:T(8,128)(2,1)S(1)} custom-call(bf16[4096,256]{1,0:T(8,128)(2,1)} %targets_ref.5), custom_call_target="tpu_custom_call" | custom-call | bytes 65536 | tf_op jit(solution)/shard_map/theirs/pallas_call | solution.py:349
  2.0 0.5 collective-permute-start.19
  2.5 1.0 %copy-done = s32[4096,32]{0,1:T(8,128)S(1)} copy-done((s32[4096,32]{0,1:T(8,128)S(1)}, s32[4096,32]{0,1:T(8,128)}, u32[]{:S(2)}) %copy-start) | copy-done | bytes 524312
  3.5 0.8 %prepare.1 = (bf16[32,2048]{1,0:T(8,128)(2,1)S(1)}, bf16[48,2048]{1,0:T(8,128)(2,1)S(1)}) custom-call(s32[32,4096]{1,0:T(8,128)S(1)} %bitcast.59, s32[32,128]{1,0:T(8,128)} %bitcast.78), custom_call_target="tpu_custom_call" | custom-call | flops 1000000000 | bytes 65536 | tf_op jit(solution)/shard_map/prepare/pallas_call | solution.py:349
  4.3 0.1 collective-permute-start.18
  4.4 0.0 copy-done.5
  4.4 0.5 collective-permute-start.20
  4.9 0.8 %collective-permute-done.18.taken_ref = bf16[32,2048]{1,0:T(8,128)(2,1)S(1)} collective-permute-done((bf16[32,2048]{1,0:T(8,128)(2,1)S(1)}, bf16[32,2048]{1,0:T(8,128)(2,1)S(1)}, u32[]{:S(2)}, u32[]{:S(2)}) %collective-permute-start.18) | collective-permute-done | bytes 131104 | tf_op jit(solution)/shard_map/ppermute | solution.py:330
  5.7 0.0 copy-done.13
  5.7 2.0 %order.2 = (s32[16,128]{1,0:T(8,128)S(1)}, s32[1]{0:T(128)}, bf16[1024,2048]{1,0:T(8,128)(2,1)S(1)}, bf16[64,1024]{1,0:T(8,128)(2,1)S(1)}) custom-call(s32[1]{0:T(128)} %constant.43.clone.1.turn_ref, s32[32,128]{1,0:T(8,128)S(1)} %bitcast.76, s32[32,128]{1,0:T(8,128)S(1)} %bitcast.79, bf16[48,2048]{1,0:T(8,128)(2,1)S(1)} %get-tuple-element.192.mine_ref, ...), custom_call_target="tpu_custom_call" | custom-call | flops 3000000000 | bytes 65536 | tf_op jit(solution)/shard_map/order/pallas_call | solution.py:349
  7.8 2.7 %collective-permute-start.21 = (bf16[64,1024]{1,0:T(8,128)(2,1)S(1)}, bf16[64,1024]{1,0:T(8,128)(2,1)S(1)}, u32[]{:S(2)}, u32[]{:S(2)}) collective-permute-start(bf16[64,1024]{1,0:T(8,128)(2,1)S(1)} %get-tuple-element.198), channel_id=1, source_target_pairs={{0,2},{1,3},{2,0},{3,1},{4,6},{5,7},{6,4},{7,5},{8,10},{9,11},{10,... | collective-permute-start | bytes 393224 | tf_op jit(solution)/shard_map/ppermute | solution.py:330
  10.5 0.0 collective-permute-done.20.o1_ref
  10.5 0.0 collective-permute-done.19.t1_ref
  10.5 5.6 %send.2 = (s16[512,256]{1,0:T(8,128)(2,1)S(1)}, s16[512,256]{1,0:T(8,128)(2,1)S(1)}, s32[1]{0:T(128)}) custom-call(s32[1]{0:T(128)} %get-tuple-element.194.rounds_ref, bf16[1024,2048]{1,0:T(8,128)(2,1)S(1)} %get-tuple-element.195.pick_ref, bf16[4096,256]{1,0:T(8,128)(2,1)S(1)} %copy-done.1, bf16[2048,256]{1,0:T(8,128)(2,1)S(1)} %collective-permute-done.19.t1_ref, ...), custom_call_target="tpu_custom_call" | custom-call | flops 4000000000 | bytes 65536 | tf_op jit(solution)/shard_map/send/pallas_call | solution.py:349
  16.1 0.1 collective-permute-start.22
  16.2 0.0 collective-permute-done.21.refs_0_
  16.2 2.2 %codes.2 = (bf16[1024,2048]{1,0:T(8,128)(2,1)S(1)}, bf16[144,256]{1,0:T(8,128)(2,1)S(1)}, bf16[144,256]{1,0:T(8,128)(2,1)S(1)}, bf16[144,256]{1,0:T(8,128)(2,1)S(1)}, bf16[144,256]{1,0:T(8,128)(2,1)S(1)}) custom-call(s32[1]{0:T(128)} %constant.43.clone.1.turn_ref, s32[1]{0:T(128)} %get-tuple-element.196.rounds_ref, ...), custom_call_target="tpu_custom_call" | custom-call | flops 3000000000 | bytes 65536 | tf_op jit(solution)/shard_map/codes/pallas_call | solution.py:349
  18.4 2.1 %collective-permute-start.23 = (bf16[144,256]{1,0:T(8,128)(2,1)S(1)}, bf16[144,256]{1,0:T(8,128)(2,1)S(1)}, u32[]{:S(2)}, u32[]{:S(2)}) collective-permute-start(bf16[144,256]{1,0:T(8,128)(2,1)S(1)} %get-tuple-element.202), channel_id=1, source_target_pairs={{0,8},{4,12},{8,0},{12,4},{16,24},{20,28},{24,16},{28,20},{1,9},{5... | collective-permute-start | bytes 221192 | tf_op jit(solution)/shard_map/ppermute | solution.py:330
  20.5 2.6 %collective-permute-start.24 = (bf16[144,256]{1,0:T(8,128)(2,1)S(1)}, bf16[144,256]{1,0:T(8,128)(2,1)S(1)}, u32[]{:S(2)}, u32[]{:S(2)}) collective-permute-start(bf16[144,256]{1,0:T(8,128)(2,1)S(1)} %get-tuple-element.203), channel_id=1, source_target_pairs={{0,16},{4,20},{8,24},{12,28},{16,0},{20,4},{24,8},{28,12},{1,17},{... | collective-permute-start | bytes 221192 | tf_op jit(solution)/shard_map/ppermute | solution.py:330
  23.1 0.0 collective-permute-start.25
  23.1 1.7 %collective-permute-start.34 = (s16[512,256]{1,0:T(8,128)(2,1)S(1)}, s16[512,256]{1,0:T(8,128)(2,1)S(1)}, u32[]{:S(2)}, u32[]{:S(2)}) collective-permute-start(s16[512,256]{1,0:T(8,128)(2,1)S(1)} %get-tuple-element.208), channel_id=1, source_target_pairs={{0,2},{1,3},{2,0},{3,1},{4,6},{5,7},{6,4},{7,5},{8,10},{9,11},{10,... | collective-permute-start | bytes 786440 | tf_op jit(solution)/shard_map/ppermute | solution.py:330
  24.9 5.0 %keep.2.own_ref = f32[1024,256]{1,0:T(8,128)S(1)} custom-call(bf16[1024,2048]{1,0:T(8,128)(2,1)S(1)} %get-tuple-element.199.pick_ref, bf16[4096,256]{1,0:T(8,128)(2,1)S(1)} %copy-done.1, bf16[2048,256]{1,0:T(8,128)(2,1)S(1)} %collective-permute-done.19.t1_ref, bf16[256,256]{1,0:T(8,128)(2,1)S(1)} %copy-done.5, ...), custom_call_target="tpu_custom_call" | custom-call | flops 4000000000 | bytes 65536 | tf_op jit(solution)/shard_map/keep/pallas_call | solution.py:349
  29.9 0.0 collective-permute-done.23.refs_2_
  29.9 0.0 collective-permute-done.24.refs_3_
  29.9 0.0 collective-permute-done.25.refs_4_
  29.9 0.0 collective-permute-done.22.refs_0_
  29.9 0.5 cosine.4
  30.5 0.1 collective-permute-done.34.refs_0_
  30.6 0.5 cosine.5
  31.0 1.1 %collective-permute-start.35 = (bf16[256,256]{1,0:T(8,128)(2,1)S(1)}, bf16[256,256]{1,0:T(8,128)(2,1)S(1)}, u32[]{:S(2)}, u32[]{:S(2)}) collective-permute-start(bf16[256,256]{1,0:T(8,128)(2,1)S(1)} %get-tuple-element.210), channel_id=1, source_target_pairs={{0,8},{4,12},{8,0},{12,4},{16,24},{20,28},{24,16},{28,20},{1,9},{5... | collective-permute-start | bytes 393224 | tf_op jit(solution)/shard_map/ppermute | solution.py:330
  32.2 0.1 collective-permute-start.26
  32.3 3.1 %collective-permute-start.29 = (bf16[256,256]{1,0:T(8,128)(2,1)S(1)}, bf16[256,256]{1,0:T(8,128)(2,1)S(1)}, u32[]{:S(2)}, u32[]{:S(2)}) collective-permute-start(bf16[256,256]{1,0:T(8,128)(2,1)S(1)} %get-tuple-element.206), channel_id=1, source_target_pairs={{0,16},{4,20},{8,24},{12,28},{16,0},{20,4},{24,8},{28,12},{1,17},{... | collective-permute-start | bytes 393224 | tf_op jit(solution)/shard_map/ppermute | solution.py:330
  35.4 0.3 collective-permute-start.30
  35.7 0.4 collective-permute-done.35
  36.1 1.6 %collective-permute-start.37 = (bf16[512,256]{1,0:T(8,128)(2,1)S(1)}, bf16[512,256]{1,0:T(8,128)(2,1)S(1)}, u32[]{:S(2)}, u32[]{:S(2)}) collective-permute-start(bf16[512,256]{1,0:T(8,128)(2,1)S(1)} %constant_dynamic-update-slice_fusion.14.refs_4_), channel_id=1, source_target_pairs={{0,4},{4,0},{8,12},{12,8},{16,20},{20,16},{24,28},{28,24},{1,5},{5... | collective-permute-start | bytes 786440 | tf_op jit(solution)/shard_map/ppermute | solution.py:330
  37.7 0.6 collective-permute-start.27
  38.3 6.9 %collective-permute-done.29 = bf16[256,256]{1,0:T(8,128)(2,1)S(1)} collective-permute-done((bf16[256,256]{1,0:T(8,128)(2,1)S(1)}, bf16[256,256]{1,0:T(8,128)(2,1)S(1)}, u32[]{:S(2)}, u32[]{:S(2)}) %collective-permute-start.29) | collective-permute-done | bytes 131104 | tf_op jit(solution)/shard_map/ppermute | solution.py:330
  45.2 0.0 collective-permute-start.36
  45.2 0.0 collective-permute-done.30
  45.3 1.6 %collective-permute-start.32 = (bf16[512,256]{1,0:T(8,128)(2,1)S(1)}, bf16[512,256]{1,0:T(8,128)(2,1)S(1)}, u32[]{:S(2)}, u32[]{:S(2)}) collective-permute-start(bf16[512,256]{1,0:T(8,128)(2,1)S(1)} %constant_dynamic-update-slice_fusion.12.refs_4_), channel_id=1, source_target_pairs={{0,4},{4,0},{8,12},{12,8},{16,20},{20,16},{24,28},{28,24},{1,5},{5... | collective-permute-start | bytes 786440 | tf_op jit(solution)/shard_map/ppermute | solution.py:330
  46.8 0.0 collective-permute-done.37.refs_6_
  46.8 0.2 collective-permute-start.38
  47.1 0.3 collective-permute-done.27
  47.4 0.1 collective-permute-start.28
  47.5 0.0 collective-permute-done.26.refs_1_
  47.5 0.5 collective-permute-start.31
  48.0 6.1 %collective-permute-done.32.refs_6_ = bf16[512,256]{1,0:T(8,128)(2,1)S(1)} collective-permute-done((bf16[512,256]{1,0:T(8,128)(2,1)S(1)}, bf16[512,256]{1,0:T(8,128)(2,1)S(1)}, u32[]{:S(2)}, u32[]{:S(2)}) %collective-permute-start.32) | collective-permute-done | bytes 262176 | tf_op jit(solution)/shard_map/ppermute | solution.py:330
  54.0 0.0 collective-permute-start.33
  54.0 0.0 collective-permute-done.28.refs_3_
  54.0 0.0 collective-permute-done.36.refs_5_
  54.0 0.0 collective-permute-done.38.refs_7_
  54.1 1.5 %sums.2 = (f32[1024,256]{1,0:T(8,128)S(1)}, f32[1024,128]{1,0:T(8,128)S(1)}) custom-call(bf16[48,1024]{1,0:T(8,128)(2,1)S(1)} %get-tuple-element.274.refs_0_, bf16[48,1024]{1,0:T(8,128)(2,1)S(1)} %collective-permute-done.26.refs_1_, bf16[48,1024]{1,0:T(8,128)(2,1)S(1)} %get-tuple-element.272.refs_2_, bf16[48,1024]{1,0:T(8,128)(2,1)S(1)} %collective-permute-done.28.refs_3_, ...), custom_call_target="tpu_custom_call" | custom-call | flops 4000000000 | bytes 65536 | tf_op jit(solution)/shard_map/sums/pallas_call | solution.py:349
  55.5 0.0 collective-permute-done.31.refs_5_
  55.6 0.0 collective-permute-done.33.refs_7_
  55.6 0.0 copy-start.12
  55.6 0.0 copy-start.14
  55.6 0.0 copy-start.16
  55.6 2.7 %gains.2 = (f32[1024,256]{1,0:T(8,128)S(1)}, f32[1024,128]{1,0:T(8,128)S(1)}, f32[32,1,128]{2,1,0:T(1,128)S(1)}, s32[1]{0:T(128)}) custom-call(bf16[48,1024]{1,0:T(8,128)(2,1)S(1)} %get-tuple-element.274.refs_0_, bf16[48,1024]{1,0:T(8,128)(2,1)S(1)} %collective-permute-done.26.refs_1_, ...), custom_call_target="tpu_custom_call", output_to_operand_aliasing={{0}: (8, {}), {1}: (9, {})} | custom-call | flops 4000000000 | bytes 65536 | tf_op jit(solution)/shard_map/gains/pallas_call | solution.py:349
  59.0 0.3 conditional.1
  59.3 12.4 %all_to_all.5.got_ref = f32[32,1,128]{2,1,0:T(1,128)S(1)} all-to-all(f32[32,1,128]{2,1,0:T(1,128)S(1)} %bitcast.74), channel_id=1, replica_groups=mesh['rows'=8,'feat'=4] {'rows','feat'}, dimensions={0} | all-to-all | bytes 32768 | tf_op jit(solution)/shard_map/all_to_all | solution.py:458
  71.7 0.7 finish.1
  (36 shorter events, 0.2 us)
Async XLA Ops:
  0.6 5.1 %copy-start.13 = (s32[4096]{0:T(1024)S(1)}, s32[4096]{0:T(1024)}, u32[]{:S(2)}) copy-start(s32[4096]{0:T(1024)} %param.15) | copy-start | bytes 49156
  0.6 3.8 %copy-start.5 = (bf16[256,256]{1,0:T(8,128)(2,1)S(1)}, bf16[256,256]{1,0:T(8,128)(2,1)}, u32[]{:S(2)}) copy-start(bf16[256,256]{1,0:T(8,128)(2,1)} %o0_ref.3) | copy-start | bytes 393220
  0.7 5.1 %copy-start.11 = (s32[4096]{0:T(1024)S(1)}, s32[4096]{0:T(1024)}, u32[]{:S(2)}) copy-start(s32[4096]{0:T(1024)} %param.14) | copy-start | bytes 49156
  2.0 8.5 %collective-permute-start.19 = (bf16[2048,256]{1,0:T(8,128)(2,1)S(1)}, bf16[2048,256]{1,0:T(8,128)(2,1)S(1)}, u32[]{:S(2)}, u32[]{:S(2)}) collective-permute-start(bf16[2048,256]{1,0:T(8,128)(2,1)S(1)} %theirs.1), channel_id=1, source_target_pairs={{0,1},{1,0},{2,3},{3,2},{4,5},{5,4},{6,7},{7,6},{8,9},{9,8},{10,11... | collective-permute-start | bytes 3145736 | tf_op jit(solution)/shard_map/ppermute | solution.py:330
  2.5 1.0 %copy-start = (s32[4096,32]{0,1:T(8,128)S(1)}, s32[4096,32]{0,1:T(8,128)}, u32[]{:S(2)}) copy-start(s32[4096,32]{0,1:T(8,128)} %param.13) | copy-start | bytes 1572868
  4.3 11.9 %copy-start.17 = (bf16[48,2048]{1,0:T(8,128)(2,1)}, bf16[48,2048]{1,0:T(8,128)(2,1)S(1)}, u32[]{:S(2)}) copy-start(bf16[48,2048]{1,0:T(8,128)(2,1)S(1)} %get-tuple-element.192.mine_ref) | copy-start | bytes 589828
  4.3 1.4 %collective-permute-start.18 = (bf16[32,2048]{1,0:T(8,128)(2,1)S(1)}, bf16[32,2048]{1,0:T(8,128)(2,1)S(1)}, u32[]{:S(2)}, u32[]{:S(2)}) collective-permute-start(bf16[32,2048]{1,0:T(8,128)(2,1)S(1)} %get-tuple-element.193), channel_id=1, source_target_pairs={{0,1},{1,0},{2,3},{3,2},{4,5},{5,4},{6,7},{7,6},{8,9},{9,8},{10,11... | collective-permute-start | bytes 393224 | tf_op jit(solution)/shard_map/ppermute | solution.py:330
  4.4 6.1 %collective-permute-start.20 = (bf16[256,256]{1,0:T(8,128)(2,1)S(1)}, bf16[256,256]{1,0:T(8,128)(2,1)S(1)}, u32[]{:S(2)}, u32[]{:S(2)}) collective-permute-start(bf16[256,256]{1,0:T(8,128)(2,1)S(1)} %copy-done.5), channel_id=1, source_target_pairs={{0,1},{1,0},{2,3},{3,2},{4,5},{5,4},{6,7},{7,6},{8,9},{9,8},{10,11... | collective-permute-start | bytes 393224 | tf_op jit(solution)/shard_map/ppermute | solution.py:330
  5.7 10.5 %copy-start.7 = (bf16[32,2048]{1,0:T(8,128)(2,1)}, bf16[32,2048]{1,0:T(8,128)(2,1)S(1)}, u32[]{:S(2)}) copy-start(bf16[32,2048]{1,0:T(8,128)(2,1)S(1)} %collective-permute-done.18.taken_ref) | copy-start | bytes 393220
  5.7 4.8 %copy-start.1 = (bf16[4096,256]{1,0:T(8,128)(2,1)S(1)}, bf16[4096,256]{1,0:T(8,128)(2,1)}, u32[]{:S(2)}) copy-start(bf16[4096,256]{1,0:T(8,128)(2,1)} %targets_ref.5) | copy-start | bytes 6291460
  7.8 8.4 %collective-permute-start.21 = (bf16[64,1024]{1,0:T(8,128)(2,1)S(1)}, bf16[64,1024]{1,0:T(8,128)(2,1)S(1)}, u32[]{:S(2)}, u32[]{:S(2)}) collective-permute-start(bf16[64,1024]{1,0:T(8,128)(2,1)S(1)} %get-tuple-element.198), channel_id=1, source_target_pairs={{0,2},{1,3},{2,0},{3,1},{4,6},{5,7},{6,4},{7,5},{8,10},{9,11},{10,... | collective-permute-start | bytes 393224 | tf_op jit(solution)/shard_map/ppermute | solution.py:330
  10.5 14.4 %copy-start.9 = (bf16[256,256]{1,0:T(8,128)(2,1)}, bf16[256,256]{1,0:T(8,128)(2,1)S(1)}, u32[]{:S(2)}) copy-start(bf16[256,256]{1,0:T(8,128)(2,1)S(1)} %collective-permute-done.20.o1_ref) | copy-start | bytes 393220
  10.5 14.4 %copy-start.3 = (bf16[2048,256]{1,0:T(8,128)(2,1)}, bf16[2048,256]{1,0:T(8,128)(2,1)S(1)}, u32[]{:S(2)}) copy-start(bf16[2048,256]{1,0:T(8,128)(2,1)S(1)} %collective-permute-done.19.t1_ref) | copy-start | bytes 3145732
  16.1 13.8 %collective-permute-start.22 = (s16[512,256]{1,0:T(8,128)(2,1)S(1)}, s16[512,256]{1,0:T(8,128)(2,1)S(1)}, u32[]{:S(2)}, u32[]{:S(2)}) collective-permute-start(s16[512,256]{1,0:T(8,128)(2,1)S(1)} %get-tuple-element.200), channel_id=1, source_target_pairs={{0,2},{1,3},{2,0},{3,1},{4,6},{5,7},{6,4},{7,5},{8,10},{9,11},{10,... | collective-permute-start | bytes 786440 | tf_op jit(solution)/shard_map/ppermute | solution.py:330
  18.4 11.5 %collective-permute-start.23 = (bf16[144,256]{1,0:T(8,128)(2,1)S(1)}, bf16[144,256]{1,0:T(8,128)(2,1)S(1)}, u32[]{:S(2)}, u32[]{:S(2)}) collective-permute-start(bf16[144,256]{1,0:T(8,128)(2,1)S(1)} %get-tuple-element.202), channel_id=1, source_target_pairs={{0,8},{4,12},{8,0},{12,4},{16,24},{20,28},{24,16},{28,20},{1,9},{5... | collective-permute-start | bytes 221192 | tf_op jit(solution)/shard_map/ppermute | solution.py:330
  20.5 9.3 %collective-permute-start.24 = (bf16[144,256]{1,0:T(8,128)(2,1)S(1)}, bf16[144,256]{1,0:T(8,128)(2,1)S(1)}, u32[]{:S(2)}, u32[]{:S(2)}) collective-permute-start(bf16[144,256]{1,0:T(8,128)(2,1)S(1)} %get-tuple-element.203), channel_id=1, source_target_pairs={{0,16},{4,20},{8,24},{12,28},{16,0},{20,4},{24,8},{28,12},{1,17},{... | collective-permute-start | bytes 221192 | tf_op jit(solution)/shard_map/ppermute | solution.py:330
  23.1 6.8 %collective-permute-start.25 = (bf16[144,256]{1,0:T(8,128)(2,1)S(1)}, bf16[144,256]{1,0:T(8,128)(2,1)S(1)}, u32[]{:S(2)}, u32[]{:S(2)}) collective-permute-start(bf16[144,256]{1,0:T(8,128)(2,1)S(1)} %get-tuple-element.204), channel_id=1, source_target_pairs={{0,24},{4,28},{8,16},{12,20},{16,8},{20,12},{24,0},{28,4},{1,25},{... | collective-permute-start | bytes 221192 | tf_op jit(solution)/shard_map/ppermute | solution.py:330
  23.1 7.4 %collective-permute-start.34 = (s16[512,256]{1,0:T(8,128)(2,1)S(1)}, s16[512,256]{1,0:T(8,128)(2,1)S(1)}, u32[]{:S(2)}, u32[]{:S(2)}) collective-permute-start(s16[512,256]{1,0:T(8,128)(2,1)S(1)} %get-tuple-element.208), channel_id=1, source_target_pairs={{0,2},{1,3},{2,0},{3,1},{4,6},{5,7},{6,4},{7,5},{8,10},{9,11},{10,... | collective-permute-start | bytes 786440 | tf_op jit(solution)/shard_map/ppermute | solution.py:330
  24.9 5.1 %copy-start.15 = (f32[256]{0:T(256)S(1)}, f32[256]{0:T(256)}, u32[]{:S(2)}) copy-start(f32[256]{0:T(256)} %param.12) | copy-start | bytes 3076
  31.0 5.0 %collective-permute-start.35 = (bf16[256,256]{1,0:T(8,128)(2,1)S(1)}, bf16[256,256]{1,0:T(8,128)(2,1)S(1)}, u32[]{:S(2)}, u32[]{:S(2)}) collective-permute-start(bf16[256,256]{1,0:T(8,128)(2,1)S(1)} %get-tuple-element.210), channel_id=1, source_target_pairs={{0,8},{4,12},{8,0},{12,4},{16,24},{20,28},{24,16},{28,20},{1,9},{5... | collective-permute-start | bytes 393224 | tf_op jit(solution)/shard_map/ppermute | solution.py:330
  32.2 15.3 %collective-permute-start.26 = (bf16[48,1024]{1,0:T(8,128)(2,1)S(1)}, bf16[48,1024]{1,0:T(8,128)(2,1)S(1)}, u32[]{:S(2)}, u32[]{:S(2)}) collective-permute-start(bf16[48,1024]{1,0:T(8,128)(2,1)S(1)} %get-tuple-element.273), channel_id=1, source_target_pairs={{0,1},{1,0},{2,3},{3,2},{4,5},{5,4},{6,7},{7,6},{8,9},{9,8},{10,11... | collective-permute-start | bytes 294920 | tf_op jit(solution)/shard_map/ppermute | solution.py:330
  32.3 12.9 %collective-permute-start.29 = (bf16[256,256]{1,0:T(8,128)(2,1)S(1)}, bf16[256,256]{1,0:T(8,128)(2,1)S(1)}, u32[]{:S(2)}, u32[]{:S(2)}) collective-permute-start(bf16[256,256]{1,0:T(8,128)(2,1)S(1)} %get-tuple-element.206), channel_id=1, source_target_pairs={{0,16},{4,20},{8,24},{12,28},{16,0},{20,4},{24,8},{28,12},{1,17},{... | collective-permute-start | bytes 393224 | tf_op jit(solution)/shard_map/ppermute | solution.py:330
  35.4 9.8 %collective-permute-start.30 = (bf16[256,256]{1,0:T(8,128)(2,1)S(1)}, bf16[256,256]{1,0:T(8,128)(2,1)S(1)}, u32[]{:S(2)}, u32[]{:S(2)}) collective-permute-start(bf16[256,256]{1,0:T(8,128)(2,1)S(1)} %get-tuple-element.207), channel_id=1, source_target_pairs={{0,24},{4,28},{8,16},{12,20},{16,8},{20,12},{24,0},{28,4},{1,25},{... | collective-permute-start | bytes 393224 | tf_op jit(solution)/shard_map/ppermute | solution.py:330
  36.1 10.7 %collective-permute-start.37 = (bf16[512,256]{1,0:T(8,128)(2,1)S(1)}, bf16[512,256]{1,0:T(8,128)(2,1)S(1)}, u32[]{:S(2)}, u32[]{:S(2)}) collective-permute-start(bf16[512,256]{1,0:T(8,128)(2,1)S(1)} %constant_dynamic-update-slice_fusion.14.refs_4_), channel_id=1, source_target_pairs={{0,4},{4,0},{8,12},{12,8},{16,20},{20,16},{24,28},{28,24},{1,5},{5... | collective-permute-start | bytes 786440 | tf_op jit(solution)/shard_map/ppermute | solution.py:330
  37.7 9.7 %collective-permute-start.27 = (bf16[80,1024]{1,0:T(8,128)(2,1)S(1)}, bf16[80,1024]{1,0:T(8,128)(2,1)S(1)}, u32[]{:S(2)}, u32[]{:S(2)}) collective-permute-start(bf16[80,1024]{1,0:T(8,128)(2,1)S(1)} %pad_maximum_fusion.6), channel_id=1, source_target_pairs={{0,4},{4,0},{8,12},{12,8},{16,20},{20,16},{24,28},{28,24},{1,5},{5... | collective-permute-start | bytes 491528 | tf_op jit(solution)/shard_map/ppermute | solution.py:330
  45.2 8.8 %collective-permute-start.36 = (bf16[512,256]{1,0:T(8,128)(2,1)S(1)}, bf16[512,256]{1,0:T(8,128)(2,1)S(1)}, u32[]{:S(2)}, u32[]{:S(2)}) collective-permute-start(bf16[512,256]{1,0:T(8,128)(2,1)S(1)} %constant_dynamic-update-slice_fusion.14.refs_4_), channel_id=1, source_target_pairs={{0,1},{1,0},{2,3},{3,2},{4,5},{5,4},{6,7},{7,6},{8,9},{9,8},{10,11... | collective-permute-start | bytes 786440 | tf_op jit(solution)/shard_map/ppermute | solution.py:330
  45.3 8.8 %collective-permute-start.32 = (bf16[512,256]{1,0:T(8,128)(2,1)S(1)}, bf16[512,256]{1,0:T(8,128)(2,1)S(1)}, u32[]{:S(2)}, u32[]{:S(2)}) collective-permute-start(bf16[512,256]{1,0:T(8,128)(2,1)S(1)} %constant_dynamic-update-slice_fusion.12.refs_4_), channel_id=1, source_target_pairs={{0,4},{4,0},{8,12},{12,8},{16,20},{20,16},{24,28},{28,24},{1,5},{5... | collective-permute-start | bytes 786440 | tf_op jit(solution)/shard_map/ppermute | solution.py:330
  46.8 7.2 %collective-permute-start.38 = (bf16[512,256]{1,0:T(8,128)(2,1)S(1)}, bf16[512,256]{1,0:T(8,128)(2,1)S(1)}, u32[]{:S(2)}, u32[]{:S(2)}) collective-permute-start(bf16[512,256]{1,0:T(8,128)(2,1)S(1)} %collective-permute-done.37.refs_6_), channel_id=1, source_target_pairs={{0,1},{1,0},{2,3},{3,2},{4,5},{5,4},{6,7},{7,6},{8,9},{9,8},{10,11... | collective-permute-start | bytes 786440 | tf_op jit(solution)/shard_map/ppermute | solution.py:330
  47.4 6.6 %collective-permute-start.28 = (bf16[48,1024]{1,0:T(8,128)(2,1)S(1)}, bf16[48,1024]{1,0:T(8,128)(2,1)S(1)}, u32[]{:S(2)}, u32[]{:S(2)}) collective-permute-start(bf16[48,1024]{1,0:T(8,128)(2,1)S(1)} %get-tuple-element.271), channel_id=1, source_target_pairs={{0,1},{1,0},{2,3},{3,2},{4,5},{5,4},{6,7},{7,6},{8,9},{9,8},{10,11... | collective-permute-start | bytes 294920 | tf_op jit(solution)/shard_map/ppermute | solution.py:330
  47.5 8.1 %collective-permute-start.31 = (bf16[512,256]{1,0:T(8,128)(2,1)S(1)}, bf16[512,256]{1,0:T(8,128)(2,1)S(1)}, u32[]{:S(2)}, u32[]{:S(2)}) collective-permute-start(bf16[512,256]{1,0:T(8,128)(2,1)S(1)} %constant_dynamic-update-slice_fusion.12.refs_4_), channel_id=1, source_target_pairs={{0,1},{1,0},{2,3},{3,2},{4,5},{5,4},{6,7},{7,6},{8,9},{9,8},{10,11... | collective-permute-start | bytes 786440 | tf_op jit(solution)/shard_map/ppermute | solution.py:330
  54.0 1.5 %collective-permute-start.33 = (bf16[512,256]{1,0:T(8,128)(2,1)S(1)}, bf16[512,256]{1,0:T(8,128)(2,1)S(1)}, u32[]{:S(2)}, u32[]{:S(2)}) collective-permute-start(bf16[512,256]{1,0:T(8,128)(2,1)S(1)} %collective-permute-done.32.refs_6_), channel_id=1, source_target_pairs={{0,1},{1,0},{2,3},{3,2},{4,5},{5,4},{6,7},{7,6},{8,9},{9,8},{10,11... | collective-permute-start | bytes 786440 | tf_op jit(solution)/shard_map/ppermute | solution.py:330
  55.6 3.4 %copy-start.6 = (bf16[256,256]{1,0:T(8,128)(2,1)S(1)}, bf16[256,256]{1,0:T(8,128)(2,1)}, u32[]{:S(2)}) copy-start(bf16[256,256]{1,0:T(8,128)(2,1)} %o0_ref.3) | copy-start | bytes 393220
  55.6 3.4 %copy-start.8 = (bf16[32,2048]{1,0:T(8,128)(2,1)S(1)}, bf16[32,2048]{1,0:T(8,128)(2,1)}, u32[]{:S(2)}) copy-start(bf16[32,2048]{1,0:T(8,128)(2,1)} %copy-done.7) | copy-start | bytes 393220
  55.6 3.4 %copy-start.10 = (bf16[256,256]{1,0:T(8,128)(2,1)S(1)}, bf16[256,256]{1,0:T(8,128)(2,1)}, u32[]{:S(2)}) copy-start(bf16[256,256]{1,0:T(8,128)(2,1)} %copy-done.9) | copy-start | bytes 393220
  55.6 3.4 %copy-start.12 = (s32[4096]{0:T(1024)S(1)}, s32[4096]{0:T(1024)}, u32[]{:S(2)}) copy-start(s32[4096]{0:T(1024)} %param.14) | copy-start | bytes 49156
  55.6 3.4 %copy-start.14 = (s32[4096]{0:T(1024)S(1)}, s32[4096]{0:T(1024)}, u32[]{:S(2)}) copy-start(s32[4096]{0:T(1024)} %param.15) | copy-start | bytes 49156
  55.6 3.4 %copy-start.16 = (f32[256]{0:T(256)S(1)}, f32[256]{0:T(256)}, u32[]{:S(2)}) copy-start(f32[256]{0:T(256)} %param.12) | copy-start | bytes 3076
  55.6 3.4 %copy-start.18 = (bf16[48,2048]{1,0:T(8,128)(2,1)S(1)}, bf16[48,2048]{1,0:T(8,128)(2,1)}, u32[]{:S(2)}) copy-start(bf16[48,2048]{1,0:T(8,128)(2,1)} %copy-done.17) | copy-start | bytes 589828

commit v3 on v2

v3 whole, which is shorter than its diff:
```python
import functools
import math

import jax
import jax.numpy as jnp
from jax import lax
from jax.experimental import pallas as pl
from jax.experimental.pallas import tpu as pltpu
from jax.sharding import PartitionSpec as P

BINS = 32
NODES = 8
LANES = 128
CHUNKS = 4
EXTRA = 16
STEPS = 65536.0
PARAMS = pltpu.CompilerParams(vmem_limit_bytes=24 * 1024 * 1024)
VMEM = pl.BlockSpec(memory_space=pltpu.VMEM)
SMEM = pl.BlockSpec(memory_space=pltpu.SMEM)
HBM = pl.BlockSpec(memory_space=pltpu.HBM)
ANY = pl.BlockSpec(memory_space=pl.ANY)


def rank_of(node, live):
    groups = node.shape[0]
    block = groups * LANES
    members = [jnp.where((node == n) & live, 1.0, 0.0) for n in range(NODES)]
    member = jnp.concatenate(members, axis=0)
    size = NODES * groups
    i = lax.broadcasted_iota(jnp.int32, (LANES, LANES), 0)
    j = lax.broadcasted_iota(jnp.int32, (LANES, LANES), 1)
    before = jnp.where(i < j, 1.0, 0.0).astype(jnp.bfloat16)
    inside = jnp.dot(member.astype(jnp.bfloat16), before, preferred_element_type=jnp.float32)
    count = jnp.sum(member, axis=1, keepdims=True)
    p = lax.broadcasted_iota(jnp.int32, (size, size), 0)
    q = lax.broadcasted_iota(jnp.int32, (size, size), 1)
    earlier = jnp.where((p // groups == q // groups) & (q < p), 1.0, 0.0).astype(jnp.bfloat16)
    spread = jnp.broadcast_to(count, (size, LANES))
    base = jnp.dot(earlier, spread.astype(jnp.bfloat16), preferred_element_type=jnp.float32)
    rank = inside + base
    pos = jnp.zeros((groups, LANES), jnp.float32)
    for n in range(NODES):
        pos += members[n] * (rank[n * groups : (n + 1) * groups] + float(n * block))
    return jnp.where(live, pos, -1.0).astype(jnp.int32), jnp.max(base + spread).astype(jnp.int32)


def choose_rows(pos_ref, pick, distance, slots, room, x, a, turn):
    groups = pos_ref.shape[0]
    block = groups * LANES
    for slot in range(slots):
        node = (x ^ distance) * slots + (a ^ slot)
        wanted = lax.broadcasted_iota(jnp.int32, (room, LANES), 0) + turn * room + node * block
        for g in range(groups):
            pick[slot * room : (slot + 1) * room, g * LANES : (g + 1) * LANES] = jnp.where(
                pos_ref[g : g + 1, :] == wanted, 1.0, 0.0
            ).astype(jnp.bfloat16)


def moved(codes, pick):
    return lax.dot_general(codes, pick, (((1,), (1,)), ((), ())), preferred_element_type=jnp.float32)


def major_of(place, slots):
    copies = lax.axis_size("rows") // slots
    return place >> (copies.bit_length() - 1)


def theirs_kernel(targets_ref, theirs_ref, sems):
    copy_half(targets_ref, theirs_ref, sems, 1 - (lax.axis_index("feat") & 1))


def copy_half(targets_ref, out_ref, sems, half, between=None):
    block = out_ref.shape[0]
    piece = block // CHUNKS
    pieces = []
    for i in range(CHUNKS):
        source = targets_ref.at[pl.ds(pl.multiple_of(half * block + i * piece, piece), piece), :]
        pieces.append(pltpu.make_async_copy(source, out_ref.at[pl.ds(i * piece, piece), :], sems.at[i]))
    for copy in pieces:
        copy.start()
    if between:
        between()
    for copy in pieces:
        copy.wait()


def prepare_kernel(copies, codes_ref, give_ref, mine_ref):
    block = mine_ref.shape[1]
    part = codes_ref.shape[0] // copies
    core = lax.axis_index("feat") & 1
    minor = lax.axis_index("rows") & (copies - 1)
    for out_ref, half in ((give_ref, 1 - core), (mine_ref, core)):
        rows = pl.ds(pl.multiple_of(half * block, block), block)
        parts = [codes_ref[pl.ds((minor ^ d) * part, part), rows] for d in range(copies)]
        out_ref[...] = jnp.concatenate(parts, axis=0).astype(jnp.float32).astype(jnp.bfloat16)


def order_kernel(slots, room, turn_ref, targets_ref, node_ref, boot_ref, pos_ref, rounds_ref, own_ref, *refs):
    picks, sems = refs[:-1], refs[-1]
    feat, place = lax.axis_index("feat"), lax.axis_index("rows")

    def order():
        groups = pos_ref.shape[0]
        lines = pl.ds(pl.multiple_of((feat & 1) * groups, groups), groups)
        pos, most = rank_of(node_ref[lines, :], boot_ref[lines, :] > 0)
        pos_ref[...] = pos
        rounds_ref[...] = jnp.broadcast_to((most + (room - 1)) // room, rounds_ref.shape)
        for distance, pick in enumerate(picks, 1):
            choose_rows(pos_ref, pick, distance, slots, room, feat >> 1, major_of(place, slots), turn_ref[:1, :])

    copy_half(targets_ref, own_ref, sems, feat & 1, order)


def turns_of(pick, t0_ref, t1_ref, o0_ref, o1_ref):
    s0 = jnp.dot(pick, t0_ref[...], preferred_element_type=jnp.float32).astype(jnp.bfloat16)
    s1 = jnp.dot(pick, t1_ref[...], preferred_element_type=jnp.float32).astype(jnp.bfloat16)
    partial = jnp.dot(s0, o0_ref[...], preferred_element_type=jnp.float32)
    partial += jnp.dot(s1, o1_ref[...], preferred_element_type=jnp.float32)
    turns = partial * (0.5 / math.pi)
    return turns - jnp.floor(turns)


def send_kernel(first, rounds_ref, pick_ref, t0_ref, t1_ref, o0_ref, o1_ref, before_ref, out_ref, passed_ref):
    del before_ref
    passed_ref[...] = rounds_ref[...]
    turns = turns_of(pick_ref[first : first + out_ref.shape[0], :], t0_ref, t1_ref, o0_ref, o1_ref)
    out_ref[...] = (jnp.minimum((turns * STEPS).astype(jnp.int32), 65535) - 32768).astype(jnp.int16)


def codes_kernel(chips, copies, slots, room, turn_ref, rounds_ref, pos_ref, boot_ref, *refs):
    inputs, pick, outs = refs[:chips], refs[chips], refs[chips + 1 :]
    feat, place = lax.axis_index("feat"), lax.axis_index("rows")
    choose_rows(pos_ref, pick, 0, slots, room, feat >> 1, major_of(place, slots), turn_ref[:1, :])
    features, block = inputs[0].shape[0] // 2, inputs[0].shape[1]
    groups = block // LANES
    first = pl.multiple_of((lax.axis_index("feat") & 1) * groups, groups)
    weights = boot_ref[pl.ds(first, groups), :].astype(jnp.float32)
    row = lax.broadcasted_iota(jnp.int32, (EXTRA, LANES), 0)
    extra = [jnp.where(row == 0, weights[g : g + 1, :], 0.0) for g in range(groups)]
    extra = jnp.concatenate(extra, axis=1).astype(jnp.bfloat16)
    codes = jnp.concatenate([ref[...] for ref in inputs] + [extra], axis=0)
    own = moved(codes, pick[...])
    part = features // copies
    lines = []
    for d in range(copies):
        for core in range(2):
            lines += [own[(2 * chip + core) * features + d * part :][:part] for chip in range(chips)]
            if chips * part % EXTRA:
                lines.append(jnp.zeros((-chips * part % EXTRA, own.shape[1]), jnp.float32))
    last = own[2 * chips * features :]
    line = lax.broadcasted_iota(jnp.int32, last.shape, 0)
    lines.append(jnp.where(line == 1, rounds_ref[:1, :1].astype(jnp.float32), last))
    lines = jnp.concatenate(lines, axis=0).astype(jnp.bfloat16)
    for slot, out_ref in enumerate(outs):
        out_ref[...] = lines[:, slot * room : (slot + 1) * room]


def keep_kernel(pick_ref, t0_ref, t1_ref, o0_ref, o1_ref, out_ref):
    out_ref[...] = turns_of(pick_ref[...], t0_ref, t1_ref, o0_ref, o1_ref)


def cosine_kernel(chips, first, own_ref, phase_ref, *refs):
    received, outs = refs[: chips - 1], refs[chips - 1 :]
    width = phase_ref.shape[1]
    room = outs[0].shape[0]
    scaling = math.sqrt(2.0 / width)
    series = [(-1.0) ** (k + 1) * (2 * math.pi) ** (2 * k + 1) / math.factorial(2 * k + 1) for k in range(7)]
    shift = phase_ref[...] * (0.5 / math.pi)
    for slot, out_ref in enumerate(outs):
        turns = own_ref[(first + slot) * room : (first + slot + 1) * room, :] + shift
        for ref in received:
            turns += (ref[slot * room : (slot + 1) * room, :].astype(jnp.float32) + 32768.5) * (1.0 / STEPS)
        turns = jnp.abs(turns - jnp.floor(turns + 0.5)) - 0.25
        square = turns * turns
        value = jnp.full_like(turns, series[-1])
        for term in series[-2::-1]:
            value = value * square + term
        out_ref[...] = (scaling * (value * turns)).astype(jnp.bfloat16)


def far_cosine_kernel(chips, first, pinned, rounds_ref, own_ref, phase_ref, *refs):
    refs[-1][...] = rounds_ref[...]
    cosine_kernel(chips, first, own_ref, phase_ref, *refs[: chips - 1], *refs[chips - 1 + pinned : -1])


def parts_kernel(copies, *refs):
    pieces, outs = refs[:-2], refs[-2:]
    room = pieces[0].shape[1]
    lines = (pieces[0].shape[0] - EXTRA) // copies // 2
    each = lines + EXTRA
    for slot, piece in enumerate(pieces):
        span = slice(slot * room, (slot + 1) * room)
        for d in range(copies):
            for core, out_ref in enumerate(outs):
                at = (2 * d + core) * lines
                out_ref[d * each : d * each + lines, span] = piece[at : at + lines, :]
                out_ref[d * each + lines : (d + 1) * each, span] = piece[2 * copies * lines :, :]


def after_kernel(*refs):
    pass


def gains_of(left, counts):
    whole = left[..., BINS - 1 :, :]
    total = counts[..., BINS - 1 :, :]
    other = total - counts
    differ = left * (1.0 / jnp.maximum(counts, 1.0)) - (whole - left) * (1.0 / jnp.maximum(other, 1.0))
    return (counts * other / total) * jnp.sum(differ * differ, axis=-1, keepdims=True)


def add_rows(features, plan, parcels, pieces, earlier, left_ref, counts_ref, table):
    lines = -(-features // EXTRA) * EXTRA
    codes, weights = [], []
    for (index, at, first), piece in zip(plan, pieces):
        span = slice(first, first + piece.shape[0])
        codes.append(parcels[index][at : at + lines, span].astype(jnp.float32))
        weights.append(parcels[index][at + lines : at + lines + EXTRA, span].astype(jnp.float32)[:1])
    codes, weight = jnp.concatenate(codes, axis=1), jnp.concatenate(weights, axis=1)
    length = weight.shape[1]
    threshold = lax.broadcasted_iota(jnp.int32, (BINS, length), 0).astype(jnp.float32)
    for f in range(features):
        rows = slice(f * BINS, (f + 1) * BINS)
        entry = jnp.where(codes[f : f + 1, :] <= threshold, weight, 0.0)
        table[rows, :] = entry.astype(jnp.bfloat16)
        folded = entry[:, :LANES]
        for g in range(1, length // LANES):
            folded += entry[:, g * LANES : (g + 1) * LANES]
        counts_ref[rows, :] = earlier[1][rows, :] + folded if earlier else folded
    block = jnp.concatenate([piece[...] for piece in pieces], axis=0)
    sums = jnp.dot(table[...], block, preferred_element_type=jnp.float32)
    left_ref[...] = earlier[0][...] + sums if earlier else sums


def sums_kernel(features, plan, parcels, *refs):
    pieces, earlier = refs[parcels : parcels + len(plan)], refs[parcels + len(plan) : -3]
    add_rows(features, plan, refs[:parcels], pieces, earlier, *refs[-3:])


def gains_kernel(features, plan, parcels, lines, sets, groups, chips, *refs):
    send_ref, needed_ref, left_ref, counts_ref, table = refs[-5:]
    sums_kernel(features, plan, parcels, *refs[:-5], left_ref, counts_ref, table)
    needed = 0.0
    for parcel in refs[:parcels]:
        for at in range(0, parcel.shape[0], EXTRA):
            if (at + EXTRA) % (-(-features // EXTRA) * EXTRA + EXTRA) == 0:
                flags = parcel[at : at + EXTRA, :].astype(jnp.float32)
                line = lax.broadcasted_iota(jnp.int32, flags.shape, 0)
                needed = jnp.maximum(needed, jnp.max(jnp.where(line == 1, flags, 0.0)))
    needed_ref[0] = needed.astype(jnp.int32)
    x = lax.axis_index("feat") >> 1
    columns = []
    largest = jnp.zeros((1, 1), jnp.float32)
    threshold = lax.broadcasted_iota(jnp.int32, (BINS, 1), 0)
    for f in range(features):
        rows = slice(f * BINS, (f + 1) * BINS)
        counts = jnp.sum(counts_ref[rows, :], axis=1, keepdims=True)
        column = gains_of(left_ref[rows, :], counts)
        column = jnp.where(threshold < BINS - 1, column, 0.0)
        largest = jnp.maximum(largest, jnp.max(column, axis=0, keepdims=True))
        columns.append(column)
    load = send_ref.shape[2]
    wide = load // BINS
    fill = jnp.broadcast_to(largest, (BINS, 1))
    i = lax.broadcasted_iota(jnp.int32, (load, load), 0)
    j = lax.broadcasted_iota(jnp.int32, (load, load), 1)
    for d in range(chips):
        for line in range(lines):
            first = (d * lines + line) * wide
            column = jnp.concatenate([jnp.where(threshold < BINS - 1, c, fill) for c in columns[first : first + wide]], axis=0)
            row = jnp.sum(jnp.where(i == j, column, 0.0), axis=0, keepdims=True)
            for place in range(groups):
                if place // (groups // sets) % lines == line:
                    for core in range(2):
                        send_ref[place * 2 * chips + 2 * (x ^ d) + core] = row


def finish_kernel(chips, slots, copies, lines, sets, groups, got_ref, gains_ref, best_ref, rows_ref):
    feat, place = lax.axis_index("feat"), lax.axis_index("rows")
    core = feat & 1
    per_set = groups // sets
    source = (place >> (per_set.bit_length() - 1)) >> (lines.bit_length() - 1)
    load = got_ref.shape[2]
    own, top = [], []
    for node in range(NODES):
        x, a = node // slots, node % slots
        index = lambda b, c: (a * copies + b) * 2 * chips + 2 * x + c
        own.append(got_ref[index(source, core)])
        largest = got_ref[index(0, 0)]
        for b in range(copies):
            for c in range(2):
                largest = jnp.maximum(largest, got_ref[index(b, c)])
        top.append(largest)
    own, top = jnp.concatenate(own, axis=0), jnp.concatenate(top, axis=0)
    for f in range(load // BINS):
        rows_ref[f * NODES : (f + 1) * NODES, :] = own[:, f * BINS : (f + 1) * BINS - 1]
    owned = gains_ref.shape[0]
    first = (place * owned) & (rows_ref.shape[0] - 1)
    gains_ref[...] = rows_ref[pl.ds(first, owned), :]
    i = lax.broadcasted_iota(jnp.int32, (NODES, NODES), 0)
    j = lax.broadcasted_iota(jnp.int32, (NODES, NODES), 1)
    best_ref[...] = jnp.sum(jnp.where(i == j, top[:, BINS - 1 : BINS], 0.0), axis=0, keepdims=True)


def split_rows(mesh_sizes, targets, omega, phase, codes, node, boot_counts):
    groups_all, feat_all = mesh_sizes
    chips = feat_all // 2
    slots = NODES // chips
    copies = groups_all // slots
    rows_dev, feat_dev = codes.shape
    width = omega.shape[1]
    block = rows_dev // 2
    room = block // NODES
    owned = feat_dev * NODES // groups_all
    per_owner = max(1, owned // NODES)
    sets = feat_dev // per_owner
    lines = sets // copies
    part = lines * per_owner
    features = chips * part

    feat = lax.axis_index("feat")
    x = feat // 2
    span = slots * room
    load = per_owner * BINS
    columns = targets.shape[1]

    def permute(axis, size, distance, array):
        return lax.ppermute(array, axis, [(i, i ^ distance) for i in range(size)])

    swap = functools.partial(permute, "feat", feat_all, 1)

    def along_x(distance, array):
        return permute("feat", feat_all, 2 * distance, array)

    def along_major(distance, array):
        return permute("rows", groups_all, copies * distance, array)

    def along_minor(distance, array):
        return permute("rows", groups_all, distance, array)

    def shaped(kind, *shape):
        return jax.ShapeDtypeStruct(shape, kind)

    def kernel(body, name, outs, scratch=(), micros=0.3, hbm=(), **more):
        def call(*arrays):
            ins = [SMEM if a.shape == (1,) else HBM if i in hbm else VMEM for i, a in enumerate(arrays)]
            return pl.pallas_call(
                body, out_shape=tuple(outs), in_specs=ins, scratch_shapes=list(scratch), compiler_params=PARAMS, name=name,
                out_specs=tuple(SMEM if out.shape == (1,) else VMEM for out in outs),
                cost_estimate=pl.CostEstimate(flops=int(micros * 1e9), bytes_accessed=1 << 16, transcendentals=0), **more,
            )(*arrays)

        return call

    first_round = jnp.zeros((8, LANES), jnp.int32)
    node_lines = node.reshape(rows_dev // LANES, LANES)
    boot_lines = boot_counts.reshape(rows_dev // LANES, LANES)
    token = shaped(jnp.int32, 8, LANES)
    def after(array, *others):
        return pl.pallas_call(
            after_kernel, out_shape=shaped(array.dtype, *array.shape), in_specs=[ANY] * (1 + len(others)), out_specs=ANY,
            input_output_aliases={0: 0}, compiler_params=PARAMS, name="after",
        )(array, *others)

    half = shaped(jnp.bfloat16, block, columns)
    sems = [pltpu.SemaphoreType.DMA((CHUNKS,))]
    (theirs,) = kernel(theirs_kernel, "theirs", [half], sems, hbm=(0,))(targets)
    theirs, omega_theirs = swap(theirs), swap(omega)
    def order(turn):
        outs = [shaped(jnp.int32, block // LANES, LANES), token, half] + [shaped(jnp.bfloat16, span, block)] * (chips - 1)
        return kernel(functools.partial(order_kernel, slots, room), "order", outs, sems, hbm=(1,))(
            turn, targets, node_lines, boot_lines
        )

    first_order = order(first_round)
    give, mine = kernel(
        functools.partial(prepare_kernel, copies), "prepare", [shaped(jnp.bfloat16, feat_dev, block)] * 2
    )(codes.T)
    halves = [jnp.concatenate([mine, swap(give)], axis=0)]
    halves += [along_x(d, halves[0]) for d in range(1, chips)]
    lines_part = -(-features // EXTRA) * EXTRA
    lines_all = 2 * copies * lines_part + EXTRA
    each = lines_part + EXTRA
    line = phase.reshape(1, width)
    near = slots // 2
    parts = [(0, near), (near, slots - near)]

    def one_round(turn, ordered, more):
        pos, rounds, own, *picks = ordered
        operands = (own, theirs, omega, omega_theirs)
        angles = {}
        for first, count in parts[::-1]:
            received = []
            for d in range(1, chips):
                sent, rounds = kernel(
                    functools.partial(send_kernel, first * room), "send",
                    [shaped(jnp.int16, count * room, width), token], micros=0.05,
                )(rounds, picks[d - 1], *operands, halves[0])
                received.append(along_x(d, sent))
            angles[first] = received
        pick, *pieces = kernel(
            functools.partial(codes_kernel, chips, copies, slots, room), "codes",
            [shaped(jnp.bfloat16, span, block)] + [shaped(jnp.bfloat16, lines_all, room)] * slots, micros=0.05,
        )(turn, rounds, pos, boot_lines, *halves)
        pieces = [along_major(d, pieces[d]) if d else pieces[d] for d in range(slots)]
        (own_angles,) = kernel(keep_kernel, "keep", [shaped(jnp.float32, span, width)], micros=4.0)(pick, *operands)
        pinned = pieces[1:-1]
        *far, rounds = kernel(
            functools.partial(far_cosine_kernel, chips, near, len(pinned)), "cosine_far",
            [shaped(jnp.bfloat16, room, width)] * (slots - near) + [token],
        )(rounds, own_angles, line, *angles[near], *pinned)
        stay, cross = kernel(
            functools.partial(parts_kernel, copies), "parts", [shaped(jnp.bfloat16, copies * each, span)] * 2
        )(*pieces)
        far = [along_major(near + i, f) for i, f in enumerate(far)]
        come = swap(cross)
        close = kernel(
            functools.partial(cosine_kernel, chips, 0), "cosine_near", [shaped(jnp.bfloat16, room, width)] * near
        )(own_angles, line, *angles[0])
        close = [along_major(d, f) if d else f for d, f in enumerate(close)]
        parcels = [stay[:each], come[:each]]
        for d in range(1, copies):
            both = jnp.concatenate([stay[d * each : (d + 1) * each], come[d * each : (d + 1) * each]], axis=0)
            parcels.append(along_minor(d, both))
        late = []
        for first, group in ((0, close), (near * room, far)):
            rows = jnp.concatenate(group, axis=0)
            if first:
                rows = after(rows, *parcels[2:])
            for d in range(copies):
                piece = along_minor(d, rows) if d else rows
                late += [((d and d + 1, 0, first), piece), ((d + 1, d and each, first), swap(piece))]
        sums = [shaped(jnp.float32, features * BINS, width), shaped(jnp.float32, features * BINS, LANES)]
        table = pltpu.VMEM((features * BINS, 2 * copies * (slots - near) * room), jnp.bfloat16)
        state = []
        for items in (late[: 2 * copies], late[2 * copies :]):
            plan, pieces = [item[0] for item in items], [item[1] for item in items]
            if state and not more:
                body = functools.partial(gains_kernel, features, plan, len(parcels), lines, sets, groups_all, chips)
                outs = [shaped(jnp.float32, groups_all * feat_all, 1, load), shaped(jnp.int32, 1)]
                scratch = [pltpu.VMEM(a.shape, a.dtype) for a in sums] + [table]
                return kernel(body, "gains", outs, scratch)(*parcels, *pieces, *state)
            state = kernel(functools.partial(sums_kernel, features, plan, len(parcels)), "sums", sums, [table])(
                *parcels, *pieces, *state
            )
        return state

    send, needed = one_round(first_round, first_order, False)

    def more_rounds():
        def step(state):
            turn, left, counts = state
            more_left, more_counts = one_round(turn, order(turn), True)
            return turn + 1, left + more_left, counts + more_counts

        zeros = [jnp.zeros((features * BINS, n), jnp.float32) for n in (width, LANES)]
        _, all_left, all_counts = lax.while_loop(lambda state: state[0][0, 0] < needed[0], step, (first_round, *zeros))
        tallies = jnp.sum(all_counts, axis=1).reshape(features, BINS, 1)
        gains = gains_of(all_left.reshape(features, BINS, width), tallies).reshape(chips, lines, per_owner, BINS)
        last = jnp.arange(BINS) == BINS - 1
        gains = jnp.where(last, jnp.max(jnp.where(last, 0.0, gains)), gains)
        gains = jnp.stack([lax.dynamic_index_in_dim(gains, x ^ d, 0, keepdims=False) for d in range(chips)])
        line_of = [place // (groups_all // sets) % lines for place in range(groups_all)]
        rows = jnp.stack([gains[:, line].reshape(chips, 1, load) for line in line_of])
        return jnp.broadcast_to(rows, (groups_all, chips, 2, load)).reshape(send.shape)

    send = lax.cond(needed[0] > 1, more_rounds, lambda: send)
    got = lax.all_to_all(send, ("rows", "feat"), 0, 0)
    gains, best = kernel(
        functools.partial(finish_kernel, chips, slots, copies, lines, sets, groups_all), "finish",
        [shaped(jnp.float32, owned, BINS - 1), shaped(jnp.float32, 1, NODES)],
        [pltpu.VMEM((per_owner * NODES, BINS - 1), jnp.float32)],
    )(got)
    return gains, best.reshape(NODES)


def solution(mesh):
    in_specs = (P("rows", "feat"), P("feat", None), P(), P("rows", "feat"), P("rows"), P("rows"))
    out_specs = (P(("feat", "rows"), None), P())
    sizes = (mesh.shape["rows"], mesh.shape["feat"])
    return jax.shard_map(
        functools.partial(split_rows, sizes), mesh=mesh, in_specs=in_specs, out_specs=out_specs, check_vma=False
    )
```

time: 72.7 us -> 67.9 us (0.934)
  Pallas kernels: 22.6 us -> 16.9 us
  waiting for transfers between devices: 14.7 us -> 16.4 us
    pallas_call x11 -> x13, Pallas kernels: 22.6 us -> 16.9 us  [call(): pl.pallas_call(body, out_shape=tuple(outs), in_specs=ins, scratch_shapes=...]
    ppermute x21 -> x20, waiting for transfers between devices: 14.7 us -> 16.4 us  [permute(): return lax.ppermute(array, axis, [(i, i ^ distance) for i in range(size)])]
    all_to_all x1, blocking collectives: 12.4 us -> 11.7 us  [split_rows(): got = lax.all_to_all(send, ('rows', 'feat'), 0, 0)]
    ppermute x21 -> x20, starting transfers between devices: 19.4 us -> 19.8 us  [permute(): return lax.ppermute(array, axis, [(i, i ^ distance) for i in range(size)])]
  transfers between devices with their start and end apart: 21 -> 20, of which waited for: 6 -> 7; matrix products, arithmetic and copies ran while one was open for 0% -> 0% of each run, Pallas kernels for 17% -> 13%
where the time goes in v3:
time: 67.9 us; the launch traced here: 67.7 us
  starting transfers between devices  19.8 us (29%)
  Pallas kernels  16.9 us (25%)
  waiting for transfers between devices  16.4 us (24%)
  blocking collectives  11.7 us (17%)
  between operations  1.59 us (2%)
  local copies, waits for them, and re-layouts  1.15 us (2%)
    ppermute x20, starting transfers between devices, permute(): return lax.ppermute(array, axis, [(i, i ^ distance) for i in range(size)])  19.8 us
    pallas_call x13, Pallas kernels, call(): pl.pallas_call(body, out_shape=tuple(outs), in_specs=ins, scratch_shapes=...  16.9 us
    ppermute x20, waiting for transfers between devices, permute(): return lax.ppermute(array, axis, [(i, i ^ distance) for i in range(size)])  16.4 us
    all_to_all x1, blocking collectives, split_rows(): got = lax.all_to_all(send, ('rows', 'feat'), 0, 0)  11.7 us
  transfers between devices with their start and end apart: 20, of which 7 were waited for; matrix products, arithmetic and copies ran while one was open for 0% of the time, Pallas kernels for 13%

profile of v3, /device:TPU:0, one launch (start us, length us, event | category | flops | bytes accessed | tf_op | source)
XLA Modules:
  0.0 67.7 jit_solution(10577866243435484019)
XLA Ops:
  0.6 0.0 copy-start.1
  0.6 0.0 copy-start.4
  0.7 0.0 copy-start.10
  0.7 0.0 copy-start.11
  0.7 1.4 %theirs.1 = bf16[2048,256]{1,0:T(8,128)(2,1)S(1)} custom-call(bf16[4096,256]{1,0:T(8,128)(2,1)} %targets_ref.3), custom_call_target="tpu_custom_call" | custom-call | flops 300000000 | bytes 65536 | tf_op jit(solution)/shard_map/theirs/pallas_call | solution.py:347
  2.1 0.5 collective-permute-start.16
  2.6 1.0 %copy-done = s32[4096,32]{0,1:T(8,128)S(1)} copy-done((s32[4096,32]{0,1:T(8,128)S(1)}, s32[4096,32]{0,1:T(8,128)}, u32[]{:S(2)}) %copy-start) | copy-done | bytes 524312
  3.7 0.1 collective-permute-start.18
  3.8 1.3 %collective-permute-done.18 = bf16[32,2048]{1,0:T(8,128)(2,1)S(1)} collective-permute-done((bf16[32,2048]{1,0:T(8,128)(2,1)S(1)}, bf16[32,2048]{1,0:T(8,128)(2,1)S(1)}, u32[]{:S(2)}, u32[]{:S(2)}) %collective-permute-start.18) | collective-permute-done | bytes 131104 | tf_op jit(solution)/shard_map/ppermute | solution.py:328
  5.1 0.0 copy-start.2
  5.1 2.9 %collective-permute-start.19 = (bf16[64,2048]{1,0:T(8,128)(2,1)S(1)}, bf16[64,2048]{1,0:T(8,128)(2,1)S(1)}, u32[]{:S(2)}, u32[]{:S(2)}) collective-permute-start(bf16[64,2048]{1,0:T(8,128)(2,1)S(1)} %constant_dynamic-update-slice_fusion.10.before_ref.refs_0_), channel_id=1, source_target_pairs={{0,2},{1,3},{2,0},{3,1},{4,6},{5,7},{6,4},{7,5},{8,10},{9,11},{10,... | collective-permute-start | bytes 786440 | tf_op jit(solution)/shard_map/ppermute | solution.py:328
  8.0 0.0 copy-done.4
  8.0 0.0 collective-permute-start.17
  8.0 0.0 copy-done.1
  8.0 0.0 copy-done.10
  8.0 0.0 copy-done.11
  8.1 1.7 %order.3 = (s32[16,128]{1,0:T(8,128)S(1)}, s32[8,128]{1,0:T(8,128)S(1)}, bf16[2048,256]{1,0:T(8,128)(2,1)S(1)}, bf16[1024,2048]{1,0:T(8,128)(2,1)S(1)}) custom-call(s32[8,128]{1,0:T(8,128)S(1)} %broadcast_in_dim.32.turn_ref, bf16[4096,256]{1,0:T(8,128)(2,1)S(1)} %copy-done.1, s32[32,128]{1,0:T(8,128)S(1)} %bitcast.32, s32[32,128]{1,0:T(8,128)S(1)} %bitcast.28), custom_call_target="tpu_custom_call" | custom-call | flops 300000000 | bytes 65536 | tf_op jit(solution)/shard_map/order/pallas_call | solution.py:347
  9.8 0.0 collective-permute-done.17.o1_ref
  9.8 0.0 collective-permute-done.16.t1_ref
  9.8 1.7 %send.6 = (s16[512,256]{1,0:T(8,128)(2,1)S(1)}, s32[8,128]{1,0:T(8,128)S(1)}) custom-call(s32[8,128]{1,0:T(8,128)S(1)} %get-tuple-element.188.rounds_ref, bf16[1024,2048]{1,0:T(8,128)(2,1)S(1)} %get-tuple-element.189.pick_ref, bf16[2048,256]{1,0:T(8,128)(2,1)S(1)} %get-tuple-element.190.t0_ref, bf16[2048,256]{1,0:T(8,128)(2,1)S(1)} %collective-permute-done.16.t1_ref, ...), custom_call_target="tpu_custom_call" | custom-call | flops 50000000 | bytes 65536 | tf_op jit(solution)/shard_map/send/pallas_call | solution.py:347
  11.5 1.7 %send.7 = (s16[512,256]{1,0:T(8,128)(2,1)S(1)}, s32[8,128]{1,0:T(8,128)S(1)}) custom-call(s32[8,128]{1,0:T(8,128)S(1)} %get-tuple-element.193.rounds_ref, bf16[1024,2048]{1,0:T(8,128)(2,1)S(1)} %get-tuple-element.189.pick_ref, bf16[2048,256]{1,0:T(8,128)(2,1)S(1)} %get-tuple-element.190.t0_ref, bf16[2048,256]{1,0:T(8,128)(2,1)S(1)} %collective-permute-done.16.t1_ref, ...), custom_call_target="tpu_custom_call" | custom-call | flops 50000000 | bytes 65536 | tf_op jit(solution)/shard_map/send/pallas_call | solution.py:347
  13.2 0.3 collective-permute-start.31
  13.5 1.1 %collective-permute-done.19.refs_1_ = bf16[64,2048]{1,0:T(8,128)(2,1)S(1)} collective-permute-done((bf16[64,2048]{1,0:T(8,128)(2,1)S(1)}, bf16[64,2048]{1,0:T(8,128)(2,1)S(1)}, u32[]{:S(2)}, u32[]{:S(2)}) %collective-permute-start.19) | collective-permute-done | bytes 262176 | tf_op jit(solution)/shard_map/ppermute | solution.py:328
  14.6 1.7 %codes.3 = (bf16[1024,2048]{1,0:T(8,128)(2,1)S(1)}, bf16[144,256]{1,0:T(8,128)(2,1)S(1)}, bf16[144,256]{1,0:T(8,128)(2,1)S(1)}, bf16[144,256]{1,0:T(8,128)(2,1)S(1)}, bf16[144,256]{1,0:T(8,128)(2,1)S(1)}) custom-call(s32[8,128]{1,0:T(8,128)S(1)} %broadcast_in_dim.32.turn_ref, s32[8,128]{1,0:T(8,128)S(1)} %get-tuple-element.194.rounds_ref, ...), custom_call_target="tpu_custom_call" | custom-call | flops 50000000 | bytes 65536 | tf_op jit(solution)/shard_map/codes/pallas_call | solution.py:347
  16.3 1.9 %collective-permute-start.20 = (bf16[144,256]{1,0:T(8,128)(2,1)S(1)}, bf16[144,256]{1,0:T(8,128)(2,1)S(1)}, u32[]{:S(2)}, u32[]{:S(2)}) collective-permute-start(bf16[144,256]{1,0:T(8,128)(2,1)S(1)} %get-tuple-element.197), channel_id=1, source_target_pairs={{0,8},{4,12},{8,0},{12,4},{16,24},{20,28},{24,16},{28,20},{1,9},{5... | collective-permute-start | bytes 221192 | tf_op jit(solution)/shard_map/ppermute | solution.py:328
  18.2 2.6 %collective-permute-start.21 = (bf16[144,256]{1,0:T(8,128)(2,1)S(1)}, bf16[144,256]{1,0:T(8,128)(2,1)S(1)}, u32[]{:S(2)}, u32[]{:S(2)}) collective-permute-start(bf16[144,256]{1,0:T(8,128)(2,1)S(1)} %get-tuple-element.198), channel_id=1, source_target_pairs={{0,16},{4,20},{8,24},{12,28},{16,0},{20,4},{24,8},{28,12},{1,17},{... | collective-permute-start | bytes 221192 | tf_op jit(solution)/shard_map/ppermute | solution.py:328
  20.8 0.0 collective-permute-start.22
  20.8 1.7 %collective-permute-start.25 = (s16[512,256]{1,0:T(8,128)(2,1)S(1)}, s16[512,256]{1,0:T(8,128)(2,1)S(1)}, u32[]{:S(2)}, u32[]{:S(2)}) collective-permute-start(s16[512,256]{1,0:T(8,128)(2,1)S(1)} %get-tuple-element.203), channel_id=1, source_target_pairs={{0,2},{1,3},{2,0},{3,1},{4,6},{5,7},{6,4},{7,5},{8,10},{9,11},{10,... | collective-permute-start | bytes 786440 | tf_op jit(solution)/shard_map/ppermute | solution.py:328
  22.5 0.0 copy-done.6
  22.5 3.0 %keep.3.own_ref = f32[1024,256]{1,0:T(8,128)S(1)} custom-call(bf16[1024,2048]{1,0:T(8,128)(2,1)S(1)} %get-tuple-element.202.pick_ref, bf16[2048,256]{1,0:T(8,128)(2,1)S(1)} %get-tuple-element.190.t0_ref, bf16[2048,256]{1,0:T(8,128)(2,1)S(1)} %collective-permute-done.16.t1_ref, bf16[256,256]{1,0:T(8,128)(2,1)S(1)} %copy-done.4, ...), custom_call_target="tpu_custom_call" | custom-call | flops 4000000000 | bytes 65536 | tf_op jit(solution)/shard_map/keep/pallas_call | solution.py:347
  25.5 0.0 collective-permute-done.20.refs_1_
  25.5 0.0 collective-permute-done.21.refs_2_
  25.6 1.5 %collective-permute-done.22.refs_3_ = bf16[144,256]{1,0:T(8,128)(2,1)S(1)} collective-permute-done((bf16[144,256]{1,0:T(8,128)(2,1)S(1)}, bf16[144,256]{1,0:T(8,128)(2,1)S(1)}, u32[]{:S(2)}, u32[]{:S(2)}) %collective-permute-start.22) | collective-permute-done | bytes 73760 | tf_op jit(solution)/shard_map/ppermute | solution.py:328
  27.1 0.1 collective-permute-start.23
  27.2 0.0 collective-permute-done.31.refs_0_
  27.2 0.5 cosine_near.3
  27.7 0.6 collective-permute-start.32
  28.3 0.0 collective-permute-done.25.refs_0_
  28.3 0.6 cosine_far.3
  28.9 2.1 %collective-permute-start.26 = (bf16[256,256]{1,0:T(8,128)(2,1)S(1)}, bf16[256,256]{1,0:T(8,128)(2,1)S(1)}, u32[]{:S(2)}, u32[]{:S(2)}) collective-permute-start(bf16[256,256]{1,0:T(8,128)(2,1)S(1)} %get-tuple-element.204), channel_id=1, source_target_pairs={{0,16},{4,20},{8,24},{12,28},{16,0},{20,4},{24,8},{28,12},{1,17},{... | collective-permute-start | bytes 393224 | tf_op jit(solution)/shard_map/ppermute | solution.py:328
  31.0 1.7 %collective-permute-start.27 = (bf16[256,256]{1,0:T(8,128)(2,1)S(1)}, bf16[256,256]{1,0:T(8,128)(2,1)S(1)}, u32[]{:S(2)}, u32[]{:S(2)}) collective-permute-start(bf16[256,256]{1,0:T(8,128)(2,1)S(1)} %get-tuple-element.205), channel_id=1, source_target_pairs={{0,24},{4,28},{8,16},{12,20},{16,8},{20,12},{24,0},{28,4},{1,25},{... | collective-permute-start | bytes 393224 | tf_op jit(solution)/shard_map/ppermute | solution.py:328
  32.8 0.0 collective-permute-done.23
  32.8 1.6 %collective-permute-start.24 = (bf16[96,1024]{1,0:T(8,128)(2,1)S(1)}, bf16[96,1024]{1,0:T(8,128)(2,1)S(1)}, u32[]{:S(2)}, u32[]{:S(2)}) collective-permute-start(bf16[96,1024]{1,0:T(8,128)(2,1)S(1)} %pad_maximum_fusion.4), channel_id=1, source_target_pairs={{0,4},{4,0},{8,12},{12,8},{16,20},{20,16},{24,28},{28,24},{1,5},{5... | collective-permute-start | bytes 589832 | tf_op jit(solution)/shard_map/ppermute | solution.py:328
  34.4 1.3 %collective-permute-done.32 = bf16[256,256]{1,0:T(8,128)(2,1)S(1)} collective-permute-done((bf16[256,256]{1,0:T(8,128)(2,1)S(1)}, bf16[256,256]{1,0:T(8,128)(2,1)S(1)}, u32[]{:S(2)}, u32[]{:S(2)}) %collective-permute-start.32) | collective-permute-done | bytes 131104 | tf_op jit(solution)/shard_map/ppermute | solution.py:328
  35.7 1.6 %collective-permute-start.34 = (bf16[512,256]{1,0:T(8,128)(2,1)S(1)}, bf16[512,256]{1,0:T(8,128)(2,1)S(1)}, u32[]{:S(2)}, u32[]{:S(2)}) collective-permute-start(bf16[512,256]{1,0:T(8,128)(2,1)S(1)} %constant_dynamic-update-slice_fusion.12.refs_3_), channel_id=1, source_target_pairs={{0,4},{4,0},{8,12},{12,8},{16,20},{20,16},{24,28},{28,24},{1,5},{5... | collective-permute-start | bytes 786440 | tf_op jit(solution)/shard_map/ppermute | solution.py:328
  37.3 4.5 %collective-permute-done.26 = bf16[256,256]{1,0:T(8,128)(2,1)S(1)} collective-permute-done((bf16[256,256]{1,0:T(8,128)(2,1)S(1)}, bf16[256,256]{1,0:T(8,128)(2,1)S(1)}, u32[]{:S(2)}, u32[]{:S(2)}) %collective-permute-start.26) | collective-permute-done | bytes 131104 | tf_op jit(solution)/shard_map/ppermute | solution.py:328
  41.8 0.0 collective-permute-done.27
  41.8 0.0 collective-permute-done.24.refs_1_.refs_2_
  41.9 1.6 %collective-permute-start.29 = (bf16[512,256]{1,0:T(8,128)(2,1)S(1)}, bf16[512,256]{1,0:T(8,128)(2,1)S(1)}, u32[]{:S(2)}, u32[]{:S(2)}) collective-permute-start(bf16[512,256]{1,0:T(8,128)(2,1)S(1)} %after.3.refs_3_), channel_id=1, source_target_pairs={{0,4},{4,0},{8,12},{12,8},{16,20},{20,16},{24,28},{28,24},{1,5},{5... | collective-permute-start | bytes 786440 | tf_op jit(solution)/shard_map/ppermute | solution.py:328
  43.4 0.0 collective-permute-start.33
  43.5 2.7 %collective-permute-done.34.refs_5_ = bf16[512,256]{1,0:T(8,128)(2,1)S(1)} collective-permute-done((bf16[512,256]{1,0:T(8,128)(2,1)S(1)}, bf16[512,256]{1,0:T(8,128)(2,1)S(1)}, u32[]{:S(2)}, u32[]{:S(2)}) %collective-permute-start.34) | collective-permute-done | bytes 262176 | tf_op jit(solution)/shard_map/ppermute | solution.py:328
  46.1 0.0 collective-permute-start.35
  46.1 0.5 collective-permute-start.28
  46.6 4.0 %collective-permute-done.29.refs_5_ = bf16[512,256]{1,0:T(8,128)(2,1)S(1)} collective-permute-done((bf16[512,256]{1,0:T(8,128)(2,1)S(1)}, bf16[512,256]{1,0:T(8,128)(2,1)S(1)}, u32[]{:S(2)}, u32[]{:S(2)}) %collective-permute-start.29) | collective-permute-done | bytes 262176 | tf_op jit(solution)/shard_map/ppermute | solution.py:328
  50.6 0.0 collective-permute-start.30
  50.6 0.0 collective-permute-done.33.refs_4_
  50.6 0.0 collective-permute-done.35.refs_6_
  50.6 1.5 %sums.5 = (f32[1024,256]{1,0:T(8,128)S(1)}, f32[1024,128]{1,0:T(8,128)S(1)}) custom-call(bf16[48,1024]{1,0:T(8,128)(2,1)S(1)} %get-tuple-element.256.refs_0_, bf16[48,1024]{1,0:T(8,128)(2,1)S(1)} %get-tuple-element.258.refs_1_, bf16[96,1024]{1,0:T(8,128)(2,1)S(1)} %collective-permute-done.24.refs_1_.refs_2_, ...), custom_call_target="tpu_custom_call" | custom-call | flops 300000000 | bytes 65536 | tf_op jit(solution)/shard_map/sums/pallas_call | solution.py:347
  52.1 0.0 collective-permute-done.28.refs_4_
  52.1 0.0 collective-permute-done.30.refs_6_
  52.1 2.4 %gains.1 = (f32[32,1,128]{2,1,0:T(1,128)S(1)}, s32[1]{0:T(128)}) custom-call(bf16[48,1024]{1,0:T(8,128)(2,1)S(1)} %get-tuple-element.256.refs_0_, bf16[48,1024]{1,0:T(8,128)(2,1)S(1)} %get-tuple-element.258.refs_1_, bf16[96,1024]{1,0:T(8,128)(2,1)S(1)} %collective-permute-done.24.refs_1_.refs_2_, bf16[512,256]{1,0:T(8,128)(2,1)S(1)} %after.3.refs_3_, ...), custom_call_target="tpu_custom_call" | custom-call | flops 300000000 | bytes 65536 | tf_op jit(solution)/shard_map/gains/pallas_call | solution.py:347
  55.2 0.2 conditional.1
  55.4 11.7 %all_to_all.5.got_ref = f32[32,1,128]{2,1,0:T(1,128)S(1)} all-to-all(f32[32,1,128]{2,1,0:T(1,128)S(1)} %bitcast.39), channel_id=1, replica_groups=mesh['rows'=8,'feat'=4] {'rows','feat'}, dimensions={0} | all-to-all | bytes 32768 | tf_op jit(solution)/shard_map/all_to_all | solution.py:468
  67.0 0.7 %finish.1 = (f32[32,31]{1,0:T(8,128)}, f32[1,8]{1,0:T(1,128)}) custom-call(f32[32,1,128]{2,1,0:T(1,128)S(1)} %all_to_all.5.got_ref), custom_call_target="tpu_custom_call" | custom-call | flops 300000000 | bytes 65536 | tf_op jit(solution)/shard_map/finish/pallas_call | solution.py:347
  (19 shorter events, 0.2 us)
Async XLA Ops:
  0.6 7.4 %copy-start.1 = (bf16[4096,256]{1,0:T(8,128)(2,1)S(1)}, bf16[4096,256]{1,0:T(8,128)(2,1)}, u32[]{:S(2)}) copy-start(bf16[4096,256]{1,0:T(8,128)(2,1)} %targets_ref.3) | copy-start | bytes 6291460
  0.6 7.4 %copy-start.4 = (bf16[256,256]{1,0:T(8,128)(2,1)S(1)}, bf16[256,256]{1,0:T(8,128)(2,1)}, u32[]{:S(2)}) copy-start(bf16[256,256]{1,0:T(8,128)(2,1)} %o0_ref.5) | copy-start | bytes 393220
  0.7 7.4 %copy-start.10 = (s32[4096]{0:T(1024)S(1)}, s32[4096]{0:T(1024)}, u32[]{:S(2)}) copy-start(s32[4096]{0:T(1024)} %param.15) | copy-start | bytes 49156
  0.7 7.4 %copy-start.11 = (s32[4096]{0:T(1024)S(1)}, s32[4096]{0:T(1024)}, u32[]{:S(2)}) copy-start(s32[4096]{0:T(1024)} %param.14) | copy-start | bytes 49156
  2.1 7.7 %collective-permute-start.16 = (bf16[2048,256]{1,0:T(8,128)(2,1)S(1)}, bf16[2048,256]{1,0:T(8,128)(2,1)S(1)}, u32[]{:S(2)}, u32[]{:S(2)}) collective-permute-start(bf16[2048,256]{1,0:T(8,128)(2,1)S(1)} %theirs.1), channel_id=1, source_target_pairs={{0,1},{1,0},{2,3},{3,2},{4,5},{5,4},{6,7},{7,6},{8,9},{9,8},{10,11... | collective-permute-start | bytes 3145736 | tf_op jit(solution)/shard_map/ppermute | solution.py:328
  2.6 1.0 %copy-start = (s32[4096,32]{0,1:T(8,128)S(1)}, s32[4096,32]{0,1:T(8,128)}, u32[]{:S(2)}) copy-start(s32[4096,32]{0,1:T(8,128)} %param.13) | copy-start | bytes 1572868
  3.7 1.4 %collective-permute-start.18 = (bf16[32,2048]{1,0:T(8,128)(2,1)S(1)}, bf16[32,2048]{1,0:T(8,128)(2,1)S(1)}, u32[]{:S(2)}, u32[]{:S(2)}) collective-permute-start(bf16[32,2048]{1,0:T(8,128)(2,1)S(1)} %get-tuple-element.192), channel_id=1, source_target_pairs={{0,1},{1,0},{2,3},{3,2},{4,5},{5,4},{6,7},{7,6},{8,9},{9,8},{10,11... | collective-permute-start | bytes 393224 | tf_op jit(solution)/shard_map/ppermute | solution.py:328
  5.1 9.5 %copy-start.2 = (bf16[64,2048]{1,0:T(8,128)(2,1)}, bf16[64,2048]{1,0:T(8,128)(2,1)S(1)}, u32[]{:S(2)}) copy-start(bf16[64,2048]{1,0:T(8,128)(2,1)S(1)} %constant_dynamic-update-slice_fusion.10.before_ref.refs_0_) | copy-start | bytes 786436
  5.1 9.5 %collective-permute-start.19 = (bf16[64,2048]{1,0:T(8,128)(2,1)S(1)}, bf16[64,2048]{1,0:T(8,128)(2,1)S(1)}, u32[]{:S(2)}, u32[]{:S(2)}) collective-permute-start(bf16[64,2048]{1,0:T(8,128)(2,1)S(1)} %constant_dynamic-update-slice_fusion.10.before_ref.refs_0_), channel_id=1, source_target_pairs={{0,2},{1,3},{2,0},{3,1},{4,6},{5,7},{6,4},{7,5},{8,10},{9,11},{10,... | collective-permute-start | bytes 786440 | tf_op jit(solution)/shard_map/ppermute | solution.py:328
  8.0 1.8 %collective-permute-start.17 = (bf16[256,256]{1,0:T(8,128)(2,1)S(1)}, bf16[256,256]{1,0:T(8,128)(2,1)S(1)}, u32[]{:S(2)}, u32[]{:S(2)}) collective-permute-start(bf16[256,256]{1,0:T(8,128)(2,1)S(1)} %copy-done.4), channel_id=1, source_target_pairs={{0,1},{1,0},{2,3},{3,2},{4,5},{5,4},{6,7},{7,6},{8,9},{9,8},{10,11... | collective-permute-start | bytes 393224 | tf_op jit(solution)/shard_map/ppermute | solution.py:328
  9.8 12.7 %copy-start.6 = (bf16[256,256]{1,0:T(8,128)(2,1)}, bf16[256,256]{1,0:T(8,128)(2,1)S(1)}, u32[]{:S(2)}) copy-start(bf16[256,256]{1,0:T(8,128)(2,1)S(1)} %collective-permute-done.17.o1_ref) | copy-start | bytes 393220
  13.2 14.0 %collective-permute-start.31 = (s16[512,256]{1,0:T(8,128)(2,1)S(1)}, s16[512,256]{1,0:T(8,128)(2,1)S(1)}, u32[]{:S(2)}, u32[]{:S(2)}) collective-permute-start(s16[512,256]{1,0:T(8,128)(2,1)S(1)} %get-tuple-element.206), channel_id=1, source_target_pairs={{0,2},{1,3},{2,0},{3,1},{4,6},{5,7},{6,4},{7,5},{8,10},{9,11},{10,... | collective-permute-start | bytes 786440 | tf_op jit(solution)/shard_map/ppermute | solution.py:328
  14.6 10.9 %copy-start.8 = (bf16[64,2048]{1,0:T(8,128)(2,1)}, bf16[64,2048]{1,0:T(8,128)(2,1)S(1)}, u32[]{:S(2)}) copy-start(bf16[64,2048]{1,0:T(8,128)(2,1)S(1)} %collective-permute-done.19.refs_1_) | copy-start | bytes 786436
  16.3 9.2 %collective-permute-start.20 = (bf16[144,256]{1,0:T(8,128)(2,1)S(1)}, bf16[144,256]{1,0:T(8,128)(2,1)S(1)}, u32[]{:S(2)}, u32[]{:S(2)}) collective-permute-start(bf16[144,256]{1,0:T(8,128)(2,1)S(1)} %get-tuple-element.197), channel_id=1, source_target_pairs={{0,8},{4,12},{8,0},{12,4},{16,24},{20,28},{24,16},{28,20},{1,9},{5... | collective-permute-start | bytes 221192 | tf_op jit(solution)/shard_map/ppermute | solution.py:328
  18.2 7.3 %collective-permute-start.21 = (bf16[144,256]{1,0:T(8,128)(2,1)S(1)}, bf16[144,256]{1,0:T(8,128)(2,1)S(1)}, u32[]{:S(2)}, u32[]{:S(2)}) collective-permute-start(bf16[144,256]{1,0:T(8,128)(2,1)S(1)} %get-tuple-element.198), channel_id=1, source_target_pairs={{0,16},{4,20},{8,24},{12,28},{16,0},{20,4},{24,8},{28,12},{1,17},{... | collective-permute-start | bytes 221192 | tf_op jit(solution)/shard_map/ppermute | solution.py:328
  20.8 6.3 %collective-permute-start.22 = (bf16[144,256]{1,0:T(8,128)(2,1)S(1)}, bf16[144,256]{1,0:T(8,128)(2,1)S(1)}, u32[]{:S(2)}, u32[]{:S(2)}) collective-permute-start(bf16[144,256]{1,0:T(8,128)(2,1)S(1)} %get-tuple-element.199), channel_id=1, source_target_pairs={{0,24},{4,28},{8,16},{12,20},{16,8},{20,12},{24,0},{28,4},{1,25},{... | collective-permute-start | bytes 221192 | tf_op jit(solution)/shard_map/ppermute | solution.py:328
  20.8 7.5 %collective-permute-start.25 = (s16[512,256]{1,0:T(8,128)(2,1)S(1)}, s16[512,256]{1,0:T(8,128)(2,1)S(1)}, u32[]{:S(2)}, u32[]{:S(2)}) collective-permute-start(s16[512,256]{1,0:T(8,128)(2,1)S(1)} %get-tuple-element.203), channel_id=1, source_target_pairs={{0,2},{1,3},{2,0},{3,1},{4,6},{5,7},{6,4},{7,5},{8,10},{9,11},{10,... | collective-permute-start | bytes 786440 | tf_op jit(solution)/shard_map/ppermute | solution.py:328
  22.5 4.7 %copy-start.12 = (f32[256]{0:T(256)S(1)}, f32[256]{0:T(256)}, u32[]{:S(2)}) copy-start(f32[256]{0:T(256)} %param.12) | copy-start | bytes 3076
  27.1 5.7 %collective-permute-start.23 = (bf16[96,1024]{1,0:T(8,128)(2,1)S(1)}, bf16[96,1024]{1,0:T(8,128)(2,1)S(1)}, u32[]{:S(2)}, u32[]{:S(2)}) collective-permute-start(bf16[96,1024]{1,0:T(8,128)(2,1)S(1)} %get-tuple-element.201), channel_id=1, source_target_pairs={{0,1},{1,0},{2,3},{3,2},{4,5},{5,4},{6,7},{7,6},{8,9},{9,8},{10,11... | collective-permute-start | bytes 589832 | tf_op jit(solution)/shard_map/ppermute | solution.py:328
  27.7 8.0 %collective-permute-start.32 = (bf16[256,256]{1,0:T(8,128)(2,1)S(1)}, bf16[256,256]{1,0:T(8,128)(2,1)S(1)}, u32[]{:S(2)}, u32[]{:S(2)}) collective-permute-start(bf16[256,256]{1,0:T(8,128)(2,1)S(1)} %get-tuple-element.208), channel_id=1, source_target_pairs={{0,8},{4,12},{8,0},{12,4},{16,24},{20,28},{24,16},{28,20},{1,9},{5... | collective-permute-start | bytes 393224 | tf_op jit(solution)/shard_map/ppermute | solution.py:328
  28.9 12.9 %collective-permute-start.26 = (bf16[256,256]{1,0:T(8,128)(2,1)S(1)}, bf16[256,256]{1,0:T(8,128)(2,1)S(1)}, u32[]{:S(2)}, u32[]{:S(2)}) collective-permute-start(bf16[256,256]{1,0:T(8,128)(2,1)S(1)} %get-tuple-element.204), channel_id=1, source_target_pairs={{0,16},{4,20},{8,24},{12,28},{16,0},{20,4},{24,8},{28,12},{1,17},{... | collective-permute-start | bytes 393224 | tf_op jit(solution)/shard_map/ppermute | solution.py:328
  31.0 10.8 %collective-permute-start.27 = (bf16[256,256]{1,0:T(8,128)(2,1)S(1)}, bf16[256,256]{1,0:T(8,128)(2,1)S(1)}, u32[]{:S(2)}, u32[]{:S(2)}) collective-permute-start(bf16[256,256]{1,0:T(8,128)(2,1)S(1)} %get-tuple-element.205), channel_id=1, source_target_pairs={{0,24},{4,28},{8,16},{12,20},{16,8},{20,12},{24,0},{28,4},{1,25},{... | collective-permute-start | bytes 393224 | tf_op jit(solution)/shard_map/ppermute | solution.py:328
  32.8 9.0 %collective-permute-start.24 = (bf16[96,1024]{1,0:T(8,128)(2,1)S(1)}, bf16[96,1024]{1,0:T(8,128)(2,1)S(1)}, u32[]{:S(2)}, u32[]{:S(2)}) collective-permute-start(bf16[96,1024]{1,0:T(8,128)(2,1)S(1)} %pad_maximum_fusion.4), channel_id=1, source_target_pairs={{0,4},{4,0},{8,12},{12,8},{16,20},{20,16},{24,28},{28,24},{1,5},{5... | collective-permute-start | bytes 589832 | tf_op jit(solution)/shard_map/ppermute | solution.py:328
  35.7 10.4 %collective-permute-start.34 = (bf16[512,256]{1,0:T(8,128)(2,1)S(1)}, bf16[512,256]{1,0:T(8,128)(2,1)S(1)}, u32[]{:S(2)}, u32[]{:S(2)}) collective-permute-start(bf16[512,256]{1,0:T(8,128)(2,1)S(1)} %constant_dynamic-update-slice_fusion.12.refs_3_), channel_id=1, source_target_pairs={{0,4},{4,0},{8,12},{12,8},{16,20},{20,16},{24,28},{28,24},{1,5},{5... | collective-permute-start | bytes 786440 | tf_op jit(solution)/shard_map/ppermute | solution.py:328
  41.9 8.7 %collective-permute-start.29 = (bf16[512,256]{1,0:T(8,128)(2,1)S(1)}, bf16[512,256]{1,0:T(8,128)(2,1)S(1)}, u32[]{:S(2)}, u32[]{:S(2)}) collective-permute-start(bf16[512,256]{1,0:T(8,128)(2,1)S(1)} %after.3.refs_3_), channel_id=1, source_target_pairs={{0,4},{4,0},{8,12},{12,8},{16,20},{20,16},{24,28},{28,24},{1,5},{5... | collective-permute-start | bytes 786440 | tf_op jit(solution)/shard_map/ppermute | solution.py:328
  43.4 7.1 %collective-permute-start.33 = (bf16[512,256]{1,0:T(8,128)(2,1)S(1)}, bf16[512,256]{1,0:T(8,128)(2,1)S(1)}, u32[]{:S(2)}, u32[]{:S(2)}) collective-permute-start(bf16[512,256]{1,0:T(8,128)(2,1)S(1)} %constant_dynamic-update-slice_fusion.12.refs_3_), channel_id=1, source_target_pairs={{0,1},{1,0},{2,3},{3,2},{4,5},{5,4},{6,7},{7,6},{8,9},{9,8},{10,11... | collective-permute-start | bytes 786440 | tf_op jit(solution)/shard_map/ppermute | solution.py:328
  46.1 4.5 %collective-permute-start.35 = (bf16[512,256]{1,0:T(8,128)(2,1)S(1)}, bf16[512,256]{1,0:T(8,128)(2,1)S(1)}, u32[]{:S(2)}, u32[]{:S(2)}) collective-permute-start(bf16[512,256]{1,0:T(8,128)(2,1)S(1)} %collective-permute-done.34.refs_5_), channel_id=1, source_target_pairs={{0,1},{1,0},{2,3},{3,2},{4,5},{5,4},{6,7},{7,6},{8,9},{9,8},{10,11... | collective-permute-start | bytes 786440 | tf_op jit(solution)/shard_map/ppermute | solution.py:328
  46.1 6.0 %collective-permute-start.28 = (bf16[512,256]{1,0:T(8,128)(2,1)S(1)}, bf16[512,256]{1,0:T(8,128)(2,1)S(1)}, u32[]{:S(2)}, u32[]{:S(2)}) collective-permute-start(bf16[512,256]{1,0:T(8,128)(2,1)S(1)} %after.3.refs_3_), channel_id=1, source_target_pairs={{0,1},{1,0},{2,3},{3,2},{4,5},{5,4},{6,7},{7,6},{8,9},{9,8},{10,11... | collective-permute-start | bytes 786440 | tf_op jit(solution)/shard_map/ppermute | solution.py:328
  50.6 1.5 %collective-permute-start.30 = (bf16[512,256]{1,0:T(8,128)(2,1)S(1)}, bf16[512,256]{1,0:T(8,128)(2,1)S(1)}, u32[]{:S(2)}, u32[]{:S(2)}) collective-permute-start(bf16[512,256]{1,0:T(8,128)(2,1)S(1)} %collective-permute-done.29.refs_5_), channel_id=1, source_target_pairs={{0,1},{1,0},{2,3},{3,2},{4,5},{5,4},{6,7},{7,6},{8,9},{9,8},{10,11... | collective-permute-start | bytes 786440 | tf_op jit(solution)/shard_map/ppermute | solution.py:328
